TPU v7x, 32 devices: a whole 2x2x4 slice. The times are simulated.
32 devices in a mesh: dp: 8 (over y, x, core), table: 4 (over z).
Axes of the slice: x: 2, y: 2, z: 4, core: 2. Of those that a mesh axis runs over, the one named last changes fastest.
Arguments:
- knowledge: bfloat16 [5, 4608, 768], P(None, ('dp', 'table')), may hold values from -2.390625 to 2.390625
- expr_table: bfloat16 [128, 768], replicated, may hold values from -2.390625 to 2.390625
- gene_owner: int32 [8192, 1], P(('dp', 'table')), may hold values from 0 to 31; in each aligned block of 256 rows (0 to 255, 256 to 511, ...) at most 16 rows name the same one
- gene_row: int32 [8192], P(('dp', 'table')), may hold values from 0 to 143
- expr_bin: int32 [8192], P(('dp', 'table')), may hold values from 0 to 127
- cell_lengths: int32 [256], P(('dp', 'table')), may hold values from 0 to 256, as said below
- norm1_gain: float32 [768], replicated, may hold values from 0.5 to 1.5
- norm1_bias: float32 [768], replicated, may hold values from -1.8 to 1.8
- w_query: bfloat16 [768, 768], replicated, may hold values from -0.21875 to 0.21875
- b_query: float32 [768], replicated, may hold values from -1.8 to 1.8
- w_key: bfloat16 [768, 768], replicated, may hold values from -0.21875 to 0.21875
- w_value: bfloat16 [768, 768], replicated, may hold values from -0.21875 to 0.21875
- b_value: float32 [768], replicated, may hold values from -1.8 to 1.8
- w_attn_out: bfloat16 [768, 768], replicated, may hold values from -0.875 to 0.875
- b_attn_out: float32 [768], replicated, may hold values from -1.8 to 1.8
- norm2_gain: float32 [768], replicated, may hold values from 0.5 to 1.5
- norm2_bias: float32 [768], replicated, may hold values from -1.8 to 1.8
- w_in: bfloat16 [768, 3072], replicated, may hold values from -0.21875 to 0.21875
- b_in: float32 [3072], replicated, may hold values from -1.8 to 1.8
- w_out: bfloat16 [3072, 768], replicated, may hold values from -0.109375 to 0.109375
- b_out: float32 [768], replicated, may hold values from -1.8 to 1.8
- cotangent: bfloat16 [8192, 768], P(('dp', 'table')), may hold values from -6 to 6
Outputs:
- mixed: bfloat16 [8192, 768], P(('dp', 'table'))
- knowledge_grad: float32 [5, 4608, 768], P(None, ('dp', 'table'))
- expr_table_grad: float32 [128, 768], replicated
- norm1_gain_grad: float32 [768], replicated
- norm1_bias_grad: float32 [768], replicated
- w_query_grad: float32 [768, 768], replicated
- b_query_grad: float32 [768], replicated
- w_key_grad: float32 [768, 768], replicated
- w_value_grad: float32 [768, 768], replicated
- b_value_grad: float32 [768], replicated
- w_attn_out_grad: float32 [768, 768], replicated
- b_attn_out_grad: float32 [768], replicated
- norm2_gain_grad: float32 [768], replicated
- norm2_bias_grad: float32 [768], replicated
- w_in_grad: float32 [768, 3072], replicated
- b_in_grad: float32 [3072], replicated
- w_out_grad: float32 [3072, 768], replicated
- b_out_grad: float32 [768], replicated
Inputs may be any that keep to these rules, and one draw needn't show every extreme that they name: `gene_owner`: within the rows of one device no owner index is named by more than 16 rows, and in every draw some device names some owner exactly 16 times. `cell_lengths`: the 8 entries of one device sum to at most 256; the first is positive and zeros stand only after the positive ones. In every draw some device holds a single cell of 256 tokens.
All inputs are finite; a program needn't handle non-finite values.
Results may differ from a plain program's by a relative error of at most 0.012.
Values may be sent and summed in bfloat16 or wider, within the bound.
A program may use at most 192 MiB of HBM per device.

v0:
```python
import jax
import jax.numpy as jnp
from jax import lax
from jax.sharding import PartitionSpec as P

HEADS = 12
HEAD_DIM = 64
TABLES = 5


LAYER_EPS = 1e-05
GELU_SLOPE = 0.7978845608028654
GELU_CUBIC = 0.044715
MASKED = -1e30


def gelu_tanh(pre_act):
    return (
        0.5
        * pre_act
        * (1.0 + jnp.tanh(GELU_SLOPE * (pre_act + GELU_CUBIC * pre_act * pre_act * pre_act)))
    )


def layer_norm(inputs, gain, shift):
    average = jnp.mean(inputs, axis=-1, keepdims=True)
    centred = inputs - average
    spread = jnp.mean(centred * centred, axis=-1, keepdims=True)
    return centred * lax.rsqrt(spread + LAYER_EPS) * gain + shift


def cell_masks(lengths, count):
    cell_ends = jnp.cumsum(lengths)
    places = jnp.arange(count, dtype=jnp.int32)
    segment = jnp.sum((places[:, None] >= cell_ends[None, :]).astype(jnp.int32), axis=1)
    live_mask = (places < cell_ends[-1]).astype(jnp.float32)
    return (segment, live_mask)


def local(
    knowledge,
    expr_table,
    gene_owner,
    gene_row,
    expr_bin,
    cell_lengths,
    norm1_gain,
    norm1_bias,
    w_query,
    b_query,
    w_key,
    w_value,
    b_value,
    w_attn_out,
    b_attn_out,
    norm2_gain,
    norm2_bias,
    w_in,
    b_in,
    w_out,
    b_out,
    cotangent,
):
    devices = lax.axis_size(("dp", "table"))
    tok_count = cotangent.shape[0]
    model_width = cotangent.shape[1]
    table_rows = knowledge.shape[1]
    capacity = 2 * tok_count // devices
    owner_ids = gene_owner[:, 0]
    owner_hot = (owner_ids[:, None] == jnp.arange(devices, dtype=jnp.int32)[None, :]).astype(
        jnp.int32
    )
    running = jnp.cumsum(owner_hot, axis=0) - owner_hot
    slot_rank = jnp.sum(running * owner_hot, axis=1)
    send_slot = owner_ids * capacity + slot_rank
    outgoing = jnp.full((devices * capacity,), -1, jnp.int32).at[send_slot].set(gene_row)
    outgoing = outgoing.reshape(devices, capacity)
    arrived = lax.all_to_all(outgoing, ("dp", "table"), split_axis=0, concat_axis=0, tiled=True)
    slot_count = arrived.shape[1]
    flat_ids = arrived.reshape(-1)
    row_hot = (flat_ids[:, None] == jnp.arange(table_rows, dtype=jnp.int32)[None, :]).astype(
        jnp.bfloat16
    )
    picked = jnp.einsum(
        "sr,krd->skd", row_hot, knowledge, preferred_element_type=jnp.float32
    ).astype(jnp.bfloat16)
    returned_rows = lax.all_to_all(
        picked.reshape(devices, slot_count, TABLES * model_width),
        ("dp", "table"),
        split_axis=0,
        concat_axis=0,
        tiled=True,
    )
    owner_hot_rows = row_hot.reshape(devices, slot_count, table_rows)
    own_rows = returned_rows.reshape(devices * capacity, returned_rows.shape[2])[send_slot]
    gene_part = jnp.sum(own_rows.reshape(tok_count, TABLES, model_width), axis=1, dtype=jnp.float32)
    expr_hot = (
        expr_bin[:, None] == jnp.arange(expr_table.shape[0], dtype=jnp.int32)[None, :]
    ).astype(jnp.bfloat16)
    embedded = gene_part + jnp.dot(expr_hot, expr_table, preferred_element_type=jnp.float32)
    segment, live_mask = cell_masks(cell_lengths, tok_count)
    normed1, norm1_back = jax.vjp(layer_norm, embedded, norm1_gain, norm1_bias)
    attn_in = normed1.astype(jnp.bfloat16)
    query_rows = (jnp.dot(attn_in, w_query, preferred_element_type=jnp.float32) + b_query).astype(
        jnp.bfloat16
    )
    key_rows = jnp.dot(attn_in, w_key, preferred_element_type=jnp.float32).astype(jnp.bfloat16)
    value_rows = (jnp.dot(attn_in, w_value, preferred_element_type=jnp.float32) + b_value).astype(
        jnp.bfloat16
    )
    block_rows = min(512, tok_count)
    block_count = tok_count // block_rows
    score_scale = HEAD_DIM ** (-0.5)
    key_heads = key_rows.reshape(tok_count, HEADS, HEAD_DIM)
    value_heads = value_rows.reshape(tok_count, HEADS, HEAD_DIM)
    query_blocks = query_rows.reshape(block_count, block_rows, HEADS, HEAD_DIM)
    segment_blocks = segment.reshape(block_count, block_rows)

    def block_scores(query_part, segment_part):
        scores = (
            jnp.einsum("qhd,khd->hqk", query_part, key_heads, preferred_element_type=jnp.float32)
            * score_scale
        )
        same_cell = segment_part[:, None] == segment[None, :]
        return jnp.where(same_cell[None], scores, MASKED)

    def attend_forward(inputs):
        query_part, segment_part = inputs
        scores = block_scores(query_part, segment_part)
        row_max = jnp.max(scores, axis=-1, keepdims=True)
        exp_scores = jnp.exp(scores - row_max)
        row_total = jnp.sum(exp_scores, axis=-1, keepdims=True)
        attn_probs = (exp_scores / row_total).astype(jnp.bfloat16)
        context_part = jnp.einsum(
            "hqk,khd->qhd", attn_probs, value_heads, preferred_element_type=jnp.float32
        )
        return (context_part.astype(jnp.bfloat16), row_max + jnp.log(row_total))

    context_blocks, log_totals = lax.map(attend_forward, (query_blocks, segment_blocks))
    context = context_blocks.reshape(tok_count, model_width)
    attended = jnp.dot(context, w_attn_out, preferred_element_type=jnp.float32) + b_attn_out
    hidden1 = embedded + attended
    normed2, norm2_back = jax.vjp(layer_norm, hidden1, norm2_gain, norm2_bias)
    ffn_in = normed2.astype(jnp.bfloat16)
    pre_act = jnp.dot(ffn_in, w_in, preferred_element_type=jnp.float32) + b_in
    activated, gelu_back = jax.vjp(gelu_tanh, pre_act)
    act_low = activated.astype(jnp.bfloat16)
    hidden2 = hidden1 + jnp.dot(act_low, w_out, preferred_element_type=jnp.float32) + b_out
    mixed = (hidden2 * live_mask[:, None]).astype(jnp.bfloat16)
    grad_hidden2 = cotangent.astype(jnp.float32) * live_mask[:, None]
    grad_ffn = grad_hidden2.astype(jnp.bfloat16)
    b_out_grad = jnp.sum(grad_ffn, axis=0, dtype=jnp.float32)
    w_out_grad = jnp.einsum("tf,td->fd", act_low, grad_ffn, preferred_element_type=jnp.float32)
    grad_act = jnp.einsum("td,fd->tf", grad_ffn, w_out, preferred_element_type=jnp.float32)
    grad_pre = gelu_back(grad_act)[0].astype(jnp.bfloat16)
    b_in_grad = jnp.sum(grad_pre, axis=0, dtype=jnp.float32)
    w_in_grad = jnp.einsum("td,tf->df", ffn_in, grad_pre, preferred_element_type=jnp.float32)
    grad_normed2 = jnp.einsum("tf,df->td", grad_pre, w_in, preferred_element_type=jnp.float32)
    grad_from2, norm2_gain_grad, norm2_bias_grad = norm2_back(grad_normed2)
    grad_hidden1 = grad_hidden2 + grad_from2
    grad_attn = grad_hidden1.astype(jnp.bfloat16)
    b_attn_out_grad = jnp.sum(grad_attn, axis=0, dtype=jnp.float32)
    w_attn_out_grad = jnp.einsum(
        "td,te->de", context, grad_attn, preferred_element_type=jnp.float32
    )
    grad_context = jnp.einsum(
        "te,de->td", grad_attn, w_attn_out, preferred_element_type=jnp.float32
    ).astype(jnp.bfloat16)
    grad_blocks = grad_context.reshape(block_count, block_rows, HEADS, HEAD_DIM)

    def attend_backward(carry, inputs):
        key_sum, value_sum = carry
        query_part, segment_part, log_part, grad_part = inputs
        scores = block_scores(query_part, segment_part)
        attn_probs = jnp.exp(scores - log_part)
        grad_probs = jnp.einsum(
            "qhd,khd->hqk", grad_part, value_heads, preferred_element_type=jnp.float32
        )
        value_sum = value_sum + jnp.einsum(
            "hqk,qhd->khd",
            attn_probs.astype(jnp.bfloat16),
            grad_part,
            preferred_element_type=jnp.float32,
        )
        grad_scores = attn_probs * (
            grad_probs - jnp.sum(attn_probs * grad_probs, axis=-1, keepdims=True)
        )
        grad_scores = grad_scores.astype(jnp.bfloat16)
        grad_query_part = (
            jnp.einsum("hqk,khd->qhd", grad_scores, key_heads, preferred_element_type=jnp.float32)
            * score_scale
        )
        key_sum = (
            key_sum
            + jnp.einsum(
                "hqk,qhd->khd", grad_scores, query_part, preferred_element_type=jnp.float32
            )
            * score_scale
        )
        return ((key_sum, value_sum), grad_query_part.astype(jnp.bfloat16))

    zero_heads = jnp.zeros((tok_count, HEADS, HEAD_DIM), jnp.float32)
    (key_sum, value_sum), grad_query_blocks = lax.scan(
        attend_backward,
        (zero_heads, zero_heads),
        (query_blocks, segment_blocks, log_totals, grad_blocks),
    )
    grad_query = grad_query_blocks.reshape(tok_count, model_width)
    grad_keys = key_sum.reshape(tok_count, model_width).astype(jnp.bfloat16)
    grad_values = value_sum.reshape(tok_count, model_width).astype(jnp.bfloat16)
    w_query_grad = jnp.einsum("td,te->de", attn_in, grad_query, preferred_element_type=jnp.float32)
    b_query_grad = jnp.sum(grad_query, axis=0, dtype=jnp.float32)
    w_key_grad = jnp.einsum("td,te->de", attn_in, grad_keys, preferred_element_type=jnp.float32)
    w_value_grad = jnp.einsum("td,te->de", attn_in, grad_values, preferred_element_type=jnp.float32)
    b_value_grad = jnp.sum(grad_values, axis=0, dtype=jnp.float32)
    grad_normed1 = jnp.einsum("te,de->td", grad_query, w_query, preferred_element_type=jnp.float32)
    grad_normed1 = grad_normed1 + jnp.einsum(
        "te,de->td", grad_keys, w_key, preferred_element_type=jnp.float32
    )
    grad_normed1 = grad_normed1 + jnp.einsum(
        "te,de->td", grad_values, w_value, preferred_element_type=jnp.float32
    )
    grad_from1, norm1_gain_grad, norm1_bias_grad = norm1_back(grad_normed1)
    grad_embedded = (grad_hidden1 + grad_from1).astype(jnp.bfloat16)
    expr_table_grad = jnp.einsum(
        "tb,td->bd", expr_hot, grad_embedded, preferred_element_type=jnp.float32
    )
    outgoing_grads = (
        jnp.zeros((devices * capacity, model_width), jnp.bfloat16).at[send_slot].set(grad_embedded)
    )
    arrived_grads = lax.all_to_all(
        outgoing_grads.reshape(devices, capacity, model_width),
        ("dp", "table"),
        split_axis=0,
        concat_axis=0,
        tiled=True,
    )
    table_grad = jnp.einsum(
        "gsr,gsd->rd", owner_hot_rows, arrived_grads, preferred_element_type=jnp.float32
    )
    knowledge_grad = jnp.broadcast_to(table_grad[None], (TABLES, table_rows, model_width))
    summed = lax.psum(
        (
            w_in_grad,
            b_in_grad,
            w_out_grad,
            b_out_grad,
            norm2_gain_grad,
            norm2_bias_grad,
            norm1_gain_grad,
            norm1_bias_grad,
            w_query_grad,
            b_query_grad,
            w_key_grad,
            w_value_grad,
            b_value_grad,
            w_attn_out_grad,
            b_attn_out_grad,
            expr_table_grad,
        ),
        ("dp", "table"),
    )
    ffn_terms = summed[:6]
    attn_terms = summed[6:]
    return (
        mixed,
        knowledge_grad,
        attn_terms[9],
        attn_terms[0],
        attn_terms[1],
        attn_terms[2],
        attn_terms[3],
        attn_terms[4],
        attn_terms[5],
        attn_terms[6],
        attn_terms[7],
        attn_terms[8],
        ffn_terms[4],
        ffn_terms[5],
        ffn_terms[0],
        ffn_terms[1],
        ffn_terms[2],
        ffn_terms[3],
    )


def solution(mesh):
    in_specs = (
        P(None, ("dp", "table"), None),
        P(),
        P(("dp", "table"), None),
        P(("dp", "table")),
        P(("dp", "table")),
        P(("dp", "table")),
        P(),
        P(),
        P(),
        P(),
        P(),
        P(),
        P(),
        P(),
        P(),
        P(),
        P(),
        P(),
        P(),
        P(),
        P(),
        P(("dp", "table"), None),
    )
    out_specs = (
        P(("dp", "table"), None),
        P(None, ("dp", "table"), None),
        P(),
        P(),
        P(),
        P(),
        P(),
        P(),
        P(),
        P(),
        P(),
        P(),
        P(),
        P(),
        P(),
        P(),
        P(),
        P(),
    )
    return jax.shard_map(local, mesh=mesh, in_specs=in_specs, out_specs=out_specs, check_vma=False)
```

profile of v0, /device:TPU:0, one launch (start us, length us, event | category | flops | bytes accessed | tf_op | source)
XLA Modules:
  0.0 698.4 jit_solution(7294578656699365862)
XLA Ops:
  11.9 14.3 %all_to_all.19 = s32[32,1,16]{2,1,0:T(1,128)S(1)} all-to-all(s32[32,1,16]{2,1,0:T(1,128)S(1)} %bitcast.118), channel_id=1, replica_groups=mesh['dp'=8,'table'=4] {'dp','table'}, dimensions={0} | all-to-all | bytes 4096 | tf_op jit(solution)/shard_map/all_to_all | solution.py:78
  27.5 2.6 convolution_convert_fusion
  30.0 5.2 copy.82
  35.2 9.8 %reshape.233 = bf16[32,16,3840]{2,1,0:T(8,128)(2,1)} reshape(bf16[512,5,768]{2,1,0:T(8,128)(2,1)} %copy.82) | data formatting | bytes 7864320 | tf_op jit(solution)/shard_map/reshape | solution.py:88
  45.0 3.7 all-to-all-start.1
  51.6 84.0 %all-to-all-done.1 = bf16[32,16,3840]{2,1,0:T(8,128)(2,1)} async-done(((bf16[32,16,3840]{2,1,0:T(8,128)(2,1)}), bf16[32,16,3840]{2,1,0:T(8,128)(2,1)}, u32[]{:S(2)}, u32[]{:S(2)}) %all-to-all-start.1) | async-done | bytes 3932192 | tf_op jit(solution)/shard_map/all_to_all | solution.py:87
  135.5 6.4 gather_fusion
  141.9 2.9 copy.83
  144.8 2.5 reduce_sum.240
  161.4 5.4 convert_reduce_fusion
  166.8 2.3 multiply_reduce_fusion.1
  176.2 3.4 convert_reduce_fusion.3
  183.3 1.9 fusion.58
  185.3 6.0 fusion.44
  191.3 5.3 fusion.50
  196.7 1.9 fusion.60
  198.6 1.9 fusion.59
  204.0 2.7 scatter_custom_fusion.1
  206.7 5.4 all-to-all-start.2
  212.4 50.9 %all-reduce = (f32[768]{0:T(1024)}, f32[768]{0:T(1024)}, f32[768]{0:T(1024)}, f32[768]{0:T(1024)}, f32[768]{0:T(1024)}, /*index=5*/f32[768]{0:T(1024)}, f32[768]{0:T(1024)}, f32[3072]{0:T(1024)}, f32[768]{0:T(1024)}) all-reduce(f32[768]{0:T(1024)S(1)} %get-tuple-element.77, ...), channel_id=1, replica_groups=mesh['dp'=8,'table'=4] {'dp','table'}, use_global_device_ids=true, to_apply=%region_21.22 | all-reduce | flops 9216 | bytes 73728 | tf_op jit(solution)/shard_map/psum | solution.py:242
  263.3 6.3 fusion.23
  270.1 396.6 %all-reduce.4.cloned.1.call-done = (f32[128,768]{1,0:T(8,128)}, f32[768,768]{1,0:T(8,128)}, f32[768,768]{1,0:T(8,128)}, f32[768,768]{1,0:T(8,128)}, f32[768,768]...) async-done(((f32[128,768]{1,0:T(8,128)}, f32[768,768]{1,0:T(8,128)}, f32[768,768]{1,0:T(8,128)}, f32[768,768]{1,0:T(8,128)}, f32[768,768]{1,0:T(8,128)}, ...) | async-done | bytes 28704784 | tf_op jit(solution)/shard_map/psum | solution.py:242
  678.0 9.3 %copy.115 = f32[768,3072]{1,0:T(8,128)} copy(f32[768,3072]{1,0:T(8,128)} %get-tuple-element.134) | data formatting | bytes 18874368
  687.4 3.7 copy.116
  (218 shorter events, 48.5 us)
Async XLA Ops:
  7.2 144.4 %copy-start = (bf16[768,768]{1,0:T(8,128)(2,1)S(1)}, bf16[768,768]{1,0:T(8,128)(2,1)}, u32[]{:S(2)}) copy-start(bf16[768,768]{1,0:T(8,128)(2,1)} %param.33) | copy-start | bytes 3538948
  10.3 40.5 %copy-start.57 = (s32[256,1]{0,1:T(1,128)}, s32[256,1]{0,1:T(1,128)S(1)}, u32[]{:S(2)}) copy-start(s32[256,1]{0,1:T(1,128)S(1)} %compare_select_fusion) | copy-start | bytes 3076
  26.2 9.1 %copy-start.26 = (s32[32,1,16]{2,1,0:T(1,128)}, s32[32,1,16]{2,1,0:T(1,128)S(1)}, u32[]{:S(2)}) copy-start(s32[32,1,16]{2,1,0:T(1,128)S(1)} %all_to_all.19) | copy-start | bytes 6148
  45.0 90.5 %all-to-all-start.1 = ((bf16[32,16,3840]{2,1,0:T(8,128)(2,1)}), bf16[32,16,3840]{2,1,0:T(8,128)(2,1)}, u32[]{:S(2)}, u32[]{:S(2)}) async-start(bf16[32,16,3840]{2,1,0:T(8,128)(2,1)} %reshape.233), calls=%async_computation.1 | async-start | bytes 7864320 | tf_op jit(solution)/shard_map/all_to_all | solution.py:87
  48.7 618.0 %all-reduce.4.cloned.1.call-start = ((), (), s32[]{:S(2)}) async-start(), calls=%async_computation.3 | async-start | bytes 57409536 | tf_op jit(solution)/shard_map/psum | solution.py:242
  149.6 6.1 copy-start.11
  159.4 9.7 %copy-start.37 = (f32[256]{0:T(256)}, f32[256]{0:T(256)S(1)}, u32[]{:S(2)}) copy-start(f32[256]{0:T(256)S(1)} %broadcast_multiply_fusion) | copy-start | bytes 3076
  159.7 9.4 %copy-start.43 = (f32[256]{0:T(256)}, f32[256]{0:T(256)S(1)}, u32[]{:S(2)}) copy-start(f32[256]{0:T(256)S(1)} %fusion.43) | copy-start | bytes 3076
  185.2 6.1 copy-start.23
  185.2 6.1 copy-start.29
  185.3 6.1 copy-start.31
  203.9 8.2 %copy-start.27 = (s32[32,1,16]{2,1,0:T(1,128)S(1)}, s32[32,1,16]{2,1,0:T(1,128)}, u32[]{:S(2)}) copy-start(s32[32,1,16]{2,1,0:T(1,128)} %copy-done.26) | copy-start | bytes 6148
  203.9 8.3 %copy-start.34 = (f32[12,64]{1,0:T(8,128)S(1)}, f32[12,64]{1,0:T(8,128)}, u32[]{:S(2)}) copy-start(f32[12,64]{1,0:T(8,128)} %get-tuple-element.116) | copy-start | bytes 9220
  203.9 8.4 %copy-start.41 = (f32[768]{0:T(1024)S(1)}, f32[768]{0:T(1024)}, u32[]{:S(2)}) copy-start(f32[768]{0:T(1024)} %get-tuple-element.97) | copy-start | bytes 9220
  203.9 8.4 %copy-start.42 = (f32[768]{0:T(1024)S(1)}, f32[768]{0:T(1024)}, u32[]{:S(2)}) copy-start(f32[768]{0:T(1024)} %get-tuple-element.103) | copy-start | bytes 9220
  203.9 8.4 %copy-start.45 = (f32[3072]{0:T(1024)S(1)}, f32[3072]{0:T(1024)}, u32[]{:S(2)}) copy-start(f32[3072]{0:T(1024)} %get-tuple-element.118) | copy-start | bytes 36868
  204.0 8.4 %copy-start.58 = (f32[768]{0:T(1024)S(1)}, f32[768]{0:T(1024)}, u32[]{:S(2)}) copy-start(f32[768]{0:T(1024)} %get-tuple-element.64) | copy-start | bytes 9220
  204.0 8.4 %copy-start.59 = (f32[768]{0:T(1024)S(1)}, f32[768]{0:T(1024)}, u32[]{:S(2)}) copy-start(f32[768]{0:T(1024)} %get-tuple-element.79) | copy-start | bytes 9220
  204.0 59.3 %copy-start.48 = (f32[256]{0:T(256)S(1)}, f32[256]{0:T(256)}, u32[]{:S(2)}) copy-start(f32[256]{0:T(256)} %compare_convert_fusion) | copy-start | bytes 3076
  204.0 59.3 %copy-start.63 = (f32[768]{0:T(1024)S(1)}, f32[768]{0:T(1024)}, u32[]{:S(2)}) copy-start(f32[768]{0:T(1024)} %param.42) | copy-start | bytes 9220
  206.7 62.8 %all-to-all-start.2 = ((bf16[32,16,768]{2,1,0:T(8,128)(2,1)}), bf16[32,16,768]{2,1,0:T(8,128)(2,1)S(1)}, u32[]{:S(2)}, u32[]{:S(2)}) async-start(bf16[32,16,768]{2,1,0:T(8,128)(2,1)} %bitcast.25), calls=%async_computation.2 | async-start | bytes 1572864 | tf_op jit(solution)/shard_map/all_to_all | solution.py:231
  676.6 10.7 %slice-start = ((s8[9437184]{0:T(1024)(128)(4,1)}), s8[4194304]{0:T(1024)(128)(4,1)S(1)}, s32[]{:S(2)}) async-start(s8[9437184]{0:T(1024)(128)(4,1)} %bitcast.99), calls=%async_computation.4 | async-start | bytes 8388608
  678.0 9.3 %slice-start.1 = ((s8[9437184]{0:T(1024)(128)(4,1)}), s8[4194304]{0:T(1024)(128)(4,1)S(1)}, s32[]{:S(2)}) async-start(s8[9437184]{0:T(1024)(128)(4,1)} %bitcast.99), calls=%async_computation.5 | async-start | bytes 8388608
  678.0 9.3 %slice-start.2 = ((s8[9437184]{0:T(1024)(128)(4,1)}), s8[1048576]{0:T(1024)(128)(4,1)S(1)}, s32[]{:S(2)}) async-start(s8[9437184]{0:T(1024)(128)(4,1)} %bitcast.99), calls=%async_computation.6 | async-start | bytes 2097152
  (51 other events, 125.5 us)
Sparse Core Ops, SparseCore 0:
  204.2 462.5 all-reduce.3
where the time goes:
time: 707 us; the launch traced here: 698 us
  waiting for transfers between devices  481 us (68%)
  blocking collectives  65.2 us (9%)
  local copies, waits for them, and re-layouts  62.2 us (9%)
  matrix products  54.2 us (8%)
  between operations  15.4 us (2%)
  other arithmetic  11.8 us (2%)
  starting transfers between devices  9.12 us (1%)
    psum x1, waiting for transfers between devices, local(): lax.psum((w_in_grad, b_in_grad, w_out_grad, b_out_grad, norm2_gain_grad,...  397 us
    all_to_all x1, waiting for transfers between devices, local(): lax.all_to_all(picked.reshape(devices, slot_count, TABLES * model_width),...  84 us
    psum x1, blocking collectives, local(): lax.psum((w_in_grad, b_in_grad, w_out_grad, b_out_grad, norm2_gain_grad,...  50.9 us
    unnamed x151, local copies, waits for them, and re-layouts  26.8 us
    all_to_all x1, blocking collectives, local(): lax.all_to_all(outgoing, ('dp', 'table'), split_axis=0, concat_axis=0, ti...  14.3 us
  transfers between devices with their start and end apart: 3, of which 2 were waited for; matrix products, arithmetic and copies ran while one was open for 2% of the time, Pallas kernels for 0%

commit v1 on v0

v1 whole, which is shorter than its diff:
```python
import functools
import math

import jax
import jax.numpy as jnp
from jax import lax
from jax.experimental import pallas as pl
from jax.experimental.pallas import tpu as pltpu
from jax.sharding import PartitionSpec as P

HEAD_DIM = 64
PAIR = 2 * HEAD_DIM
SCALE = HEAD_DIM ** (-0.5)
LAYER_EPS = 1e-05
GELU_SLOPE = 0.7978845608028654
GELU_CUBIC = 0.044715
MASKED = -1e30
MESH = pl.DeviceIdType.MESH
BF = jnp.bfloat16
F32 = jnp.float32
DMA = pltpu.SemaphoreType.DMA


def dot(lhs, rhs, lhs_dim=1, rhs_dim=0):
    return lax.dot_general(
        lhs, rhs, (((lhs_dim,), (rhs_dim,)), ((), ())), preferred_element_type=F32
    )


def column_sum(values):
    return jnp.sum(values, axis=0, keepdims=True)


def row_mean(values):
    return jnp.mean(values, axis=1, keepdims=True)


def standardise(values):
    centred = values - row_mean(values)
    recip = lax.rsqrt(row_mean(centred * centred) + LAYER_EPS)
    return centred * recip, recip


def norm_back(xhat, recip, gain, grad):
    scaled = gain * grad
    return recip * (scaled - row_mean(scaled) - xhat * row_mean(scaled * xhat))


class Place:
    def __init__(self, side, layers):
        self.side, self.layers = side, layers
        dp = lax.axis_index("dp")
        self.z = lax.axis_index("table")
        self.a, self.b, self.core = dp // (2 * side), (dp // 2) % side, dp % 2
        self.me = dp * layers + self.z
        self.count = 2 * side * side * layers
        self.other_core = self.at(self.a, self.b, 1 - self.core, self.z)
        self.up = self.at(self.a, self.b, self.core, jnp.minimum(self.z + 1, layers - 1))
        self.down = self.at(self.a, self.b, self.core, jnp.maximum(self.z - 1, 0))

    def at(self, a, b, core, z):
        return ((a * self.side + b) * 2 + core, z)

    def flat(self, index):
        return (index // self.layers, lax.rem(index, self.layers))

    def copy(self, src, dst, send_sem, recv_sem, to):
        return pltpu.make_async_remote_copy(
            src_ref=src,
            dst_ref=dst,
            send_sem=send_sem,
            recv_sem=recv_sem,
            device_id=to,
            device_id_type=MESH,
        )

    def send(self, src, dst, send_sem, recv_sem, to):
        self.copy(src, dst, send_sem, recv_sem, to).start()

    def arrived(self, dst, recv_sem):
        self.copy(dst, dst, recv_sem, recv_sem, self.other_core).wait_recv()

    def sent(self, src, send_sem):
        self.copy(src, src, send_sem, send_sem, self.other_core).wait_send()

    def greet_all(self):
        bar = pltpu.get_barrier_semaphore()

        def greet(step, carry):
            to = self.flat(lax.rem(self.me + step, self.count))
            pl.semaphore_signal(bar, inc=1, device_id=to, device_id_type=MESH)
            return carry

        lax.fori_loop(1, self.count, greet, 0)

    def await_all(self):
        pl.semaphore_wait(pltpu.get_barrier_semaphore(), self.count - 1)

    def exchange_start(self, out, into, send_sem, recv_sems):
        def start(step, carry):
            to = lax.rem(self.me + step, self.count)
            self.send(out.at[to], into.at[self.me], send_sem, recv_sems.at[step], self.flat(to))
            return carry

        lax.fori_loop(1, self.count, start, 0)

    def exchange_wait(self, into, recv_sems):
        def wait(step, carry):
            origin = lax.rem(self.me + self.count - step, self.count)
            self.arrived(into.at[origin], recv_sems.at[step])
            return carry

        lax.fori_loop(1, self.count, wait, 0)


class Reducer:
    def __init__(self, place, part, gath, bufs, recv, sent):
        self.p = place
        self.part, self.gath = part, gath
        self.core_buf, self.first_buf, self.z_buf, self.last_buf, self.z_sum, self.final = bufs
        (
            self.core_in,
            self.first_in,
            self.z_in,
            self.last_in,
            self.own_in,
            self.z_back,
            self.first_back,
            self.core_back,
        ) = recv
        (
            self.core_out,
            self.first_out,
            self.z_out,
            self.last_out,
            self.z_ret,
            self.first_ret,
            self.core_ret,
        ) = sent
        n = place.side
        layers = place.layers
        self.stages = (
            [self.first_sum]
            + [functools.partial(self.z_step, s) for s in range(1, layers - 1)]
            + [self.z_final, self.last_sum]
            + [functools.partial(self.z_return, s) for s in range(1, layers)]
            + [self.core_return, self.finish]
        )

    def axes(self, k):
        p = self.p
        even = lax.rem(k, 2) == 0
        first = jnp.where(even, p.b, p.a)
        last = jnp.where(even, p.a, p.b)

        def first_peer(m):
            q = lax.rem(first + m, p.side)
            return q, p.at(jnp.where(even, p.a, q), jnp.where(even, q, p.b), p.core, p.z)

        def last_peer(m):
            q = lax.rem(last + m, p.side)
            return q, p.at(jnp.where(even, q, p.a), jnp.where(even, p.b, q), p.core, p.z)

        return first, last, first_peer, last_peer

    def core_send(self, k):
        p = self.p
        p.send(
            self.part.at[k, 1 - p.core],
            self.core_buf.at[k],
            self.core_out,
            self.core_in.at[k],
            p.other_core,
        )

    def core_sum(self, k):
        p = self.p
        _, _, first_peer, _ = self.axes(k)
        p.arrived(self.core_buf.at[k], self.core_in.at[k])
        self.core_buf[k] = (
            self.core_buf[k].astype(F32) + self.part[k, p.core].astype(F32)
        ).astype(BF)
        for m in range(1, p.side):
            q, to = first_peer(m)
            p.send(
                self.core_buf.at[k, q],
                self.first_buf.at[k, m - 1],
                self.first_out,
                self.first_in.at[k, m - 1],
                to,
            )

    def first_sum(self, k):
        p = self.p
        first, _, _, _ = self.axes(k)
        for m in range(1, p.side):
            p.arrived(self.first_buf.at[k, m - 1], self.first_in.at[k, m - 1])
        total = self.core_buf[k, first].astype(F32)
        for m in range(1, p.side):
            total = total + self.first_buf[k, m - 1].astype(F32)
        self.first_buf[k, 0] = total.astype(BF)
        top = p.layers - 1

        @pl.when(p.z == 0)
        def _():
            for j in range(top, 0, -1):
                slot = j if j > 1 else p.layers
                p.send(
                    self.first_buf.at[k, 0, j],
                    self.z_buf.at[k, slot],
                    self.z_out,
                    self.z_in.at[k, slot],
                    p.up,
                )

        @pl.when(p.z == top)
        def _():
            for j in range(0, top):
                p.send(
                    self.first_buf.at[k, 0, j],
                    self.z_buf.at[k, j],
                    self.z_out,
                    self.z_in.at[k, j],
                    p.down,
                )

    def z_add(self, k, j):
        self.p.arrived(self.z_buf.at[k, j], self.z_in.at[k, j])
        self.z_buf[k, j] = (
            self.z_buf[k, j].astype(F32) + self.first_buf[k, 0, j].astype(F32)
        ).astype(BF)

    def z_step(self, s, k):
        p = self.p
        top = p.layers - 1

        @pl.when(p.z == s)
        def _():
            for j in range(top, s, -1):
                self.z_add(k, j)
                slot = j if j > s + 1 else p.layers
                p.send(
                    self.z_buf.at[k, j],
                    self.z_buf.at[k, slot],
                    self.z_out,
                    self.z_in.at[k, slot],
                    p.up,
                )

        @pl.when(p.z == top - s)
        def _():
            for j in range(0, top - s):
                self.z_add(k, j)
                p.send(
                    self.z_buf.at[k, j],
                    self.z_buf.at[k, j],
                    self.z_out,
                    self.z_in.at[k, j],
                    p.down,
                )

    def z_final(self, k):
        p = self.p
        top = p.layers - 1
        _, _, _, last_peer = self.axes(k)

        def arrival(slot):
            p.arrived(self.z_buf.at[k, slot], self.z_in.at[k, slot])
            return self.z_buf[k, slot].astype(F32)

        own = self.first_buf[k, 0, p.z].astype(F32)

        @pl.when(p.z == 0)
        def _():
            self.z_sum[k] = (own + arrival(0)).astype(BF)

        @pl.when(p.z == top)
        def _():
            self.z_sum[k] = (own + arrival(p.layers)).astype(BF)

        @pl.when((p.z > 0) & (p.z < top))
        def _():
            self.z_sum[k] = (own + arrival(p.layers) + arrival(p.z)).astype(BF)

        for m in range(1, p.side):
            _, to = last_peer(m)
            p.send(
                self.z_sum.at[k],
                self.last_buf.at[k, m - 1],
                self.last_out,
                self.last_in.at[k, m - 1],
                to,
            )

    def last_sum(self, k):
        p = self.p
        first, last, _, _ = self.axes(k)
        for m in range(1, p.side):
            p.arrived(self.last_buf.at[k, m - 1], self.last_in.at[k, m - 1])
        total = None
        for q in range(p.side):
            m = lax.rem(last - q + p.side, p.side)
            term = jnp.where(
                m == 0,
                self.z_sum[k].astype(F32),
                self.last_buf[k, jnp.maximum(m - 1, 0)].astype(F32),
            )
            total = term if total is None else total + term
        self.final[k] = total.astype(BF)
        own = self.final.at[k]
        there = self.gath.at[k, p.core, first, p.z]
        pltpu.make_async_copy(own, there, self.own_in.at[k]).start()

        @pl.when(p.z < p.layers - 1)
        def _():
            p.send(own, there, self.z_ret, self.z_back.at[k, p.z], p.up)

        @pl.when(p.z > 0)
        def _():
            p.send(own, there, self.z_ret, self.z_back.at[k, p.z], p.down)

    def z_return(self, s, k):
        p = self.p
        first, _, first_peer, _ = self.axes(k)
        top = p.layers - 1

        @pl.when(p.z >= s)
        def _():
            j = jnp.maximum(p.z - s, 0)
            shard = self.gath.at[k, p.core, first, j]
            p.arrived(shard, self.z_back.at[k, j])

            @pl.when(p.z < top)
            def _():
                p.send(shard, shard, self.z_ret, self.z_back.at[k, j], p.up)

        @pl.when(p.z <= top - s)
        def _():
            j = jnp.minimum(p.z + s, top)
            shard = self.gath.at[k, p.core, first, j]
            p.arrived(shard, self.z_back.at[k, j])

            @pl.when(p.z > 0)
            def _():
                p.send(shard, shard, self.z_ret, self.z_back.at[k, j], p.down)

        if s == top:
            own = self.final.at[k]
            pltpu.make_async_copy(
                own, self.gath.at[k, p.core, first, p.z], self.own_in.at[k]
            ).wait()
            mine = self.gath.at[k, p.core, first]
            for m in range(1, p.side):
                _, to = first_peer(m)
                p.send(mine, mine, self.first_ret, self.first_back.at[k, m - 1], to)

    def core_return(self, k):
        p = self.p
        first, _, _, _ = self.axes(k)
        for m in range(1, p.side):
            q = lax.rem(first - m + p.side, p.side)
            p.arrived(self.gath.at[k, p.core, q], self.first_back.at[k, m - 1])
        mine = self.gath.at[k, p.core]
        p.send(mine, mine, self.core_ret, self.core_back.at[k], p.other_core)

    def finish(self, k):
        p = self.p
        p.arrived(self.gath.at[k, 1 - p.core], self.core_back.at[k])

    def drain(self):
        p = self.p
        p.sent(self.core_buf, self.core_out)
        p.sent(self.first_buf, self.first_out)
        p.sent(self.z_buf.at[:, pl.ds(0, p.layers - 1)], self.z_out)
        p.sent(self.last_buf, self.last_out)
        middle = (p.z > 0) & (p.z < p.layers - 1)

        @pl.when(middle)
        def _():
            p.sent(self.z_buf, self.z_ret)

        @pl.when(jnp.logical_not(middle))
        def _():
            p.sent(self.z_buf.at[:, pl.ds(0, 1)], self.z_ret)

        p.sent(self.first_buf, self.first_ret)
        p.sent(self.core_buf, self.core_ret)


def reducer_scratch(count, side, layers, rows, wide):
    bufs = [
        pltpu.VMEM((count, side, layers, rows, wide), BF),
        pltpu.VMEM((count, side - 1, layers, rows, wide), BF),
        pltpu.VMEM((count, layers + 1, rows, wide), BF),
        pltpu.VMEM((count, side - 1, rows, wide), BF),
        pltpu.VMEM((count, rows, wide), BF),
        pltpu.VMEM((count, rows, wide), BF),
    ]
    recv = [
        DMA((count,)),
        DMA((count, side - 1)),
        DMA((count, layers + 1)),
        DMA((count, side - 1)),
        DMA((count,)),
        DMA((count, layers)),
        DMA((count, side - 1)),
        DMA((count,)),
    ]
    return bufs, recv, [DMA(())] * 7


def layer_kernel(cfg, *refs):
    refs = list(refs)

    def take(number):
        taken = refs[:number]
        del refs[:number]
        return taken

    (knowledge, expr_table, owner_ids, gene_row, expr_bin, lengths) = take(6)
    (gain1, bias1, w_query, b_query, w_key, w_value, b_value, w_out1, b_out1) = take(9)
    (gain2, bias2, w_in, b_in, w_out, b_out, cotangent) = take(7)
    mixed, table_grad, gath = take(3)
    know_v, wq_v, wk_v, wv_v, wo_v, win_v, wout_v, cot_v = take(8)
    load_sems, ids_out, ids_in, rows_out, rows_in, back_in, row_hot_v, slot_hot_v = take(8)
    ids_sem, rows_sem, ids_sent, rows_sent, back_sent = take(5)
    (embedded_v, attn_in_v, query_v, key_v, value_v, probs_v, context_v) = take(7)
    (hidden1_v, ffn_in_v, grad_ffn_v, acc_v, gn2_v, biases_v) = take(6)
    (part,) = take(1)
    bufs, recv, sent = take(6), take(8), take(7)
    assert not refs

    side, layers, cap, offsets = cfg
    place = Place(side, layers)
    devices = place.count
    red = Reducer(place, part, gath, bufs, recv, sent)
    tokens, width = embedded_v.shape
    table_rows = knowledge.shape[1]
    half = width // 2
    blocks = w_in.shape[1] // width
    count = part.shape[0]
    slots = devices * cap

    loads = [
        (knowledge, know_v),
        (w_query, wq_v),
        (w_key, wk_v),
        (w_value, wv_v),
        (w_out1, wo_v),
        (cotangent, cot_v),
    ]
    for j in range(blocks):
        loads.append((w_in.at[:, pl.ds(j * width, width)], win_v.at[j % 2]))
        loads.append((w_out.at[pl.ds(j * width, width)], wout_v.at[j % 2]))
    loads = [
        pltpu.make_async_copy(src, dst, load_sems.at[i]) for i, (src, dst) in enumerate(loads)
    ]
    for load in loads[: 6 + 4]:
        load.start()
    place.greet_all()

    def iota(shape, dim):
        return lax.broadcasted_iota(jnp.int32, shape, dim)

    def hot(condition):
        return jnp.where(condition, 1.0, 0.0).astype(BF)

    owner_row = owner_ids[...]
    owner_hot = hot(iota((devices, tokens), 0) == owner_row)
    earlier = hot(iota((tokens, tokens), 0) < iota((tokens, tokens), 1))
    before = dot(owner_hot, earlier)
    rank_row = column_sum(before * owner_hot.astype(F32)).astype(jnp.int32)
    slot_hot_v[...] = hot(iota((slots, tokens), 0) == owner_row * cap + rank_row)
    rank_hot = hot(iota((128, tokens), 0) == rank_row)
    named = (owner_hot.astype(F32) * (gene_row[...] + 1).astype(F32)).astype(BF)
    wanted = dot(named, rank_hot, 1, 1)
    for d in range(devices):
        ids_out[d] = wanted[d : d + 1]

    place.await_all()
    place.exchange_start(ids_out, ids_in, ids_sent, ids_sem)
    ids_in[place.me] = ids_out[place.me]
    loads[0].wait()
    table_sum = know_v[0].astype(F32)
    for k in range(1, know_v.shape[0]):
        table_sum = table_sum + know_v[k].astype(F32)
    table_sum = table_sum.astype(BF)
    expr_hot = hot(iota((expr_table.shape[0], tokens), 0) == expr_bin[...])
    expr_part = dot(expr_hot, expr_table[...], 0, 0)
    place.exchange_wait(ids_in, ids_sem)
    asked = ids_in[...].reshape(devices, 128).astype(BF)
    spread = hot(iota((slots, devices), 0) // cap == iota((slots, devices), 1))
    asked = dot(spread, asked)
    own_lane = lax.rem(iota((slots, 128), 0), cap) == iota((slots, 128), 1)
    asked = jnp.sum(jnp.where(own_lane, asked, 0.0), axis=1, keepdims=True)
    row_hot = hot(iota((slots, table_rows), 1) + 1 == asked.astype(jnp.int32))
    row_hot_v[...] = row_hot
    rows_out[...] = dot(row_hot, table_sum).astype(BF).reshape(devices, cap, width)
    place.exchange_start(rows_out, rows_in, rows_sent, rows_sem)
    rows_in[place.me] = rows_out[place.me]

    end = lengths[0]
    ends = [end]
    for c in range(1, lengths.shape[0]):
        end = end + lengths[c]
        ends.append(end)

    def segments(shape, dim):
        spot = iota(shape, dim)
        segment = jnp.zeros(shape, jnp.int32)
        for stop in ends:
            segment = segment + jnp.where(spot >= stop, 1, 0)
        return segment

    spot = lax.rem(iota((2 * tokens, tokens), 0), tokens)
    segment = jnp.zeros((2 * tokens, tokens), jnp.int32)
    for stop in ends:
        segment = segment + jnp.where(spot >= stop, 1, 0)
    same_cell = segment == segments((2 * tokens, tokens), 1)
    live = jnp.where(iota((tokens, 1), 0) < ends[-1], 1.0, 0.0)

    place.exchange_wait(rows_in, rows_sem)
    gathered = rows_in[...].reshape(slots, width)
    embedded_v[...] = dot(slot_hot_v[...], gathered, 0, 0) + expr_part
    for load in loads[1:5]:
        load.wait()

    xhat1, recip1 = standardise(embedded_v[...])
    attn_in_v[...] = (xhat1 * gain1[...].reshape(1, width) + bias1[...].reshape(1, width)).astype(BF)
    query_v[...] = (dot(attn_in_v[...], wq_v[...]) + b_query[...].reshape(1, width)).astype(BF)
    key_v[...] = dot(attn_in_v[...], wk_v[...]).astype(BF)
    value_v[...] = (dot(attn_in_v[...], wv_v[...]) + b_value[...].reshape(1, width)).astype(BF)
    low_lane = iota((tokens, PAIR), 1) < HEAD_DIM

    def two_heads(values):
        zero = jnp.zeros_like(values)
        return jnp.concatenate(
            [jnp.where(low_lane, values, zero), jnp.where(low_lane, zero, values)], axis=0
        )

    def one_of_two(values):
        return jnp.where(low_lane, values[:tokens], values[tokens:])

    for pair in range(width // PAIR):
        lanes = slice(pair * PAIR, (pair + 1) * PAIR)
        scores = dot(two_heads(query_v[:, lanes]), key_v[:, lanes], 1, 1) * SCALE
        scores = jnp.where(same_cell, scores, MASKED)
        scores = jnp.exp(scores - jnp.max(scores, axis=1, keepdims=True))
        probs = scores / jnp.sum(scores, axis=1, keepdims=True)
        probs_v[pair] = probs
        context_v[:, lanes] = one_of_two(dot(probs.astype(BF), value_v[:, lanes])).astype(BF)
    hidden1_v[...] = (
        embedded_v[...] + dot(context_v[...], wo_v[...]) + b_out1[...].reshape(1, width)
    )
    loads[5].wait()

    xhat2, recip2 = standardise(hidden1_v[...])
    ffn_in_v[...] = (xhat2 * gain2[...].reshape(1, width) + bias2[...].reshape(1, width)).astype(BF)
    grad_hidden2 = cot_v[...].astype(F32) * live
    grad_ffn_v[...] = grad_hidden2.astype(BF)
    acc_v[...] = jnp.zeros_like(acc_v)
    gn2_v[...] = jnp.zeros_like(gn2_v)
    biases_v[...] = jnp.zeros_like(biases_v)
    shard = part.shape[1:]

    def put(k, values):
        part[k] = values.reshape(shard).astype(BF)
        red.core_send(k)

    def put_bias(row, values):
        biases_v[pl.ds(2 * row, 1), :] = values[:, :half]
        biases_v[pl.ds(2 * row + 1, 1), :] = values[:, half:]

    for j in range(blocks):
        loads[6 + 2 * j].wait()
        loads[7 + 2 * j].wait()
        win, wout = win_v.at[j % 2], wout_v.at[j % 2]
        pre = dot(ffn_in_v[...], win[...]) + b_in[pl.ds(j * width, width)].reshape(1, width)
        square = pre * pre
        bend = jnp.tanh(GELU_SLOPE * (pre + GELU_CUBIC * square * pre))
        act = (0.5 * pre * (1.0 + bend)).astype(BF)
        slope = 0.5 * (1.0 + bend) + 0.5 * pre * (1.0 - bend * bend) * (
            GELU_SLOPE * (1.0 + 3.0 * GELU_CUBIC * square)
        )
        grad_pre = dot(grad_ffn_v[...], wout[...], 1, 1) * slope
        grad_pre = grad_pre.astype(BF)
        for h in range(2):
            put(4 * j + h, dot(act, grad_ffn_v[:, h * half : (h + 1) * half], 0, 0))
        for h in range(2):
            put(4 * j + 2 + h, dot(ffn_in_v[...], grad_pre[:, h * half : (h + 1) * half], 0, 0))
        acc_v[...] += dot(act, wout[...])
        gn2_v[...] += dot(grad_pre, win[...], 1, 1)
        if j + 2 < blocks:
            loads[10 + 2 * j].start()
            loads[11 + 2 * j].start()
        put_bias(j, column_sum(grad_pre.astype(F32)))
        if j:
            for q in range(4):
                red.core_sum(4 * (j - 1) + q)
    at = 4 * blocks
    mixed[...] = (
        (hidden1_v[...] + acc_v[...] + b_out[...].reshape(1, width)) * live
    ).astype(BF)
    put_bias(blocks, column_sum(grad_ffn_v[...].astype(F32)))
    grad_normed2 = gn2_v[...]
    put_bias(blocks + 1, column_sum(grad_normed2 * xhat2))
    put_bias(blocks + 2, column_sum(grad_normed2))
    for q in range(4):
        red.core_sum(at - 4 + q)
    grad_hidden1 = grad_hidden2 + norm_back(xhat2, recip2, gain2[...].reshape(1, width), grad_normed2)
    acc_v[...] = grad_hidden1
    grad_attn = grad_hidden1.astype(BF)
    put_bias(blocks + 3, column_sum(grad_attn.astype(F32)))
    for h in range(2):
        put(at + h, dot(context_v[...], grad_attn[:, h * half : (h + 1) * half], 0, 0))
    gctx_v = ffn_in_v
    gctx_v[...] = dot(grad_attn, wo_v[...], 1, 1).astype(BF)
    gq_v, gk_v, gv_v = query_v, key_v, value_v

    for pair in range(width // PAIR):
        lanes = slice(pair * PAIR, (pair + 1) * PAIR)
        probs = probs_v[pair]
        grads = two_heads(gctx_v[:, lanes])
        grad_probs = dot(grads, value_v[:, lanes], 1, 1)
        inner = jnp.sum(probs * grad_probs, axis=1, keepdims=True)
        grad_scores = (probs * (grad_probs - inner)).astype(BF)
        grad_query = one_of_two(dot(grad_scores, key_v[:, lanes])) * SCALE
        grad_key = dot(grad_scores, two_heads(query_v[:, lanes]), 0, 0) * SCALE
        gq_v[:, lanes] = grad_query.astype(BF)
        gk_v[:, lanes] = grad_key.astype(BF)
        gv_v[:, lanes] = dot(probs.astype(BF), grads, 0, 0).astype(BF)
    for q in range(2):
        red.core_sum(at + q)
    at += 2
    for grad in (gq_v, gk_v, gv_v):
        for h in range(2):
            put(at + h, dot(attn_in_v[...], grad[:, h * half : (h + 1) * half], 0, 0))
        at += 2
    put_bias(blocks + 4, column_sum(gq_v[...].astype(F32)))
    put_bias(blocks + 5, column_sum(gv_v[...].astype(F32)))
    grad_normed1 = dot(gq_v[...], wq_v[...], 1, 1)
    grad_normed1 = grad_normed1 + dot(gk_v[...], wk_v[...], 1, 1)
    grad_normed1 = grad_normed1 + dot(gv_v[...], wv_v[...], 1, 1)
    xhat1, recip1 = standardise(embedded_v[...])
    put_bias(blocks + 6, column_sum(grad_normed1 * xhat1))
    put_bias(blocks + 7, column_sum(grad_normed1))
    grad_embedded = acc_v[...] + norm_back(
        xhat1, recip1, gain1[...].reshape(1, width), grad_normed1
    )
    grad_embedded = grad_embedded.astype(BF)
    back_out = rows_out
    place.sent(rows_out.at[pl.ds(0, devices - 1)], rows_sent)
    back_out[...] = dot(slot_hot_v[...], grad_embedded).astype(BF).reshape(devices, cap, width)
    expr_grad = dot(expr_hot, grad_embedded)
    bins = expr_grad.shape[0]
    filler = jnp.zeros((width - 2 * bins - biases_v.shape[0], half), F32)
    put(
        at,
        jnp.concatenate([expr_grad[:, :half], expr_grad[:, half:], biases_v[...], filler], axis=0),
    )
    place.exchange_start(back_out, back_in, back_sent, ids_sem)
    back_in[place.me] = back_out[place.me]
    for k in range(at - 6, at + 1):
        red.core_sum(k)

    reach = [0]
    for offset in offsets:
        reach.append(reach[-1] + offset)
    assert len(reach) == len(red.stages)

    def step(i, carry):
        for stage, lag in reversed(list(zip(red.stages, reach))):
            k = i - lag

            @pl.when((k >= 0) & (k < count))
            def _():
                stage(k)

        return carry

    lax.fori_loop(0, count + reach[-1], step, 0)
    place.exchange_wait(back_in, ids_sem)
    table_grad[...] = dot(row_hot_v[...], back_in[...].reshape(slots, width), 0, 0)
    place.sent(ids_out.at[pl.ds(0, devices - 1)], ids_sent)
    place.sent(back_out.at[pl.ds(0, devices - 1)], back_sent)
    red.drain()


def layer(side, layers, args):
    (knowledge, expr_table, gene_owner, gene_row, expr_bin, cell_lengths) = args[:6]
    cotangent, w_in = args[21], args[17]
    tokens, width = cotangent.shape
    devices = 2 * side * side * layers
    cap = max(8, 2 * tokens // devices)
    slots = devices * cap
    table_rows = knowledge.shape[1]
    blocks = w_in.shape[1] // width
    count = 4 * blocks + 9
    half = width // 2
    shard = width // (2 * side * layers)
    whole = (count, 2, side, layers, shard, half)
    bufs, recv, sent = reducer_scratch(count, side, layers, shard, half)
    wide = lambda dtype: pltpu.VMEM((tokens, width), dtype)
    square = pltpu.VMEM((width, width), BF)
    scratch = [
        pltpu.VMEM(knowledge.shape, BF),
        square,
        square,
        square,
        square,
        pltpu.VMEM((2, width, width), BF),
        pltpu.VMEM((2, width, width), BF),
        wide(BF),
        DMA((6 + 2 * blocks,)),
        pltpu.VMEM((devices, 1, 128), F32),
        pltpu.VMEM((devices, 1, 128), F32),
        pltpu.VMEM((devices, cap, width), BF),
        pltpu.VMEM((devices, cap, width), BF),
        pltpu.VMEM((devices, cap, width), BF),
        pltpu.VMEM((slots, table_rows), BF),
        pltpu.VMEM((slots, tokens), BF),
        DMA((devices,)),
        DMA((devices,)),
        DMA(()),
        DMA(()),
        DMA(()),
        wide(F32),
        wide(BF),
        wide(BF),
        wide(BF),
        wide(BF),
        pltpu.VMEM((width // PAIR, 2 * tokens, tokens), F32),
        wide(BF),
        wide(F32),
        wide(BF),
        wide(BF),
        wide(F32),
        wide(F32),
        pltpu.VMEM((8 * ((2 * (blocks + 8) + 7) // 8), half), F32),
        pltpu.VMEM(whole, BF),
    ]
    vmem = pl.BlockSpec(memory_space=pltpu.VMEM)
    hbm = pl.BlockSpec(memory_space=pl.ANY)
    smem = pl.BlockSpec(memory_space=pltpu.SMEM)
    in_hbm = {0, 8, 10, 11, 13, 17, 19, 21}
    specs = [hbm if i in in_hbm else smem if i == 5 else vmem for i in range(22)]
    offsets = OFFSETS
    flops = 2 * tokens * (3 * (4 * width * width + 2 * width * w_in.shape[1]))
    return pl.pallas_call(
        functools.partial(layer_kernel, (side, layers, cap, offsets)),
        out_shape=(
            jax.ShapeDtypeStruct((tokens, width), BF),
            jax.ShapeDtypeStruct((table_rows, width), F32),
            jax.ShapeDtypeStruct(whole, BF),
        ),
        in_specs=specs,
        out_specs=(vmem, vmem, hbm),
        scratch_shapes=scratch + bufs + recv + sent,
        compiler_params=pltpu.CompilerParams(
            collective_id=1, has_side_effects=True, vmem_limit_bytes=VMEM_BYTES
        ),
        cost_estimate=pl.CostEstimate(flops=flops, bytes_accessed=40 << 20, transcendentals=0),
    )(
        knowledge,
        expr_table,
        gene_owner.reshape(1, tokens),
        gene_row.reshape(1, tokens),
        expr_bin.reshape(1, tokens),
        *args[5:],
    )


OFFSETS = [2, 2, 2, 2, 2, 2, 2, 3, 1]
VMEM_BYTES = 62 << 20
DEPTH = 4


def spread_kernel(gath, table_grad, *refs):
    (know_out, expr_out, gain1_out, bias1_out, wq_out, bq_out, wk_out, wv_out, bv_out) = refs[:9]
    (wo_out, bo1_out, gain2_out, bias2_out, win_out, bin_out, wout_out, bout_out) = refs[9:17]
    narrow, broad, in_sems, out_sems, know_sems = refs[17:]
    count, width, half = gath.shape
    blocks = win_out.shape[1] // width
    places = []
    for j in range(blocks):
        rows = pl.ds(j * width, width)
        for h in range(2):
            places.append(wout_out.at[rows, pl.ds(h * half, half)])
        for h in range(2):
            places.append(win_out.at[:, pl.ds(j * width + h * half, half)])
    for out in (wo_out, wq_out, wk_out, wv_out):
        for h in range(2):
            places.append(out.at[:, pl.ds(h * half, half)])
    assert len(places) == count - 1

    def fetch(k):
        return pltpu.make_async_copy(gath.at[k], narrow.at[k % DEPTH], in_sems.at[k % DEPTH])

    def store(k):
        return pltpu.make_async_copy(broad.at[k % DEPTH], places[k], out_sems.at[k % DEPTH])

    for k in range(DEPTH - 1):
        fetch(k).start()
    knows = [
        pltpu.make_async_copy(table_grad, know_out.at[i], know_sems.at[i])
        for i in range(know_out.shape[0])
    ]
    for know in knows:
        know.start()
    for k in range(count):
        if k + DEPTH - 1 < count:
            fetch(k + DEPTH - 1).start()
        fetch(k).wait()
        if k == count - 1:
            break
        if k >= DEPTH:
            store(k - DEPTH).wait()
        broad[k % DEPTH] = narrow[k % DEPTH].astype(F32)
        store(k).start()
    small = narrow.at[(count - 1) % DEPTH]
    bins = expr_out.shape[0]
    expr_out[:, :half] = small[pl.ds(0, bins), :].astype(F32)
    expr_out[:, half:] = small[pl.ds(bins, bins), :].astype(F32)
    biases = small[pl.ds(2 * bins, 8 * ((2 * (blocks + 8) + 7) // 8)), :].astype(F32)

    def bias(i):
        return jnp.concatenate([biases[2 * i : 2 * i + 1], biases[2 * i + 1 : 2 * i + 2]], axis=1)[0]

    for j in range(blocks):
        bin_out[pl.ds(j * width, width)] = bias(j)
    for i, out in enumerate(
        (bout_out, gain2_out, bias2_out, bo1_out, bq_out, bv_out, gain1_out, bias1_out)
    ):
        out[...] = bias(blocks + i)
    for k in range(max(0, count - 1 - DEPTH), count - 1):
        store(k).wait()
    for know in knows:
        know.wait()


def spread(gath, table_grad, tables, bins, hidden):
    count, width, half = gath.shape
    shape = lambda *dims: jax.ShapeDtypeStruct(dims, F32)
    vector, square = shape(width), shape(width, width)
    vmem = pl.BlockSpec(memory_space=pltpu.VMEM)
    hbm = pl.BlockSpec(memory_space=pl.ANY)
    outs = (
        (shape(tables, *table_grad.shape), hbm),
        (shape(bins, width), vmem),
        (vector, vmem),
        (vector, vmem),
        (square, hbm),
        (vector, vmem),
        (square, hbm),
        (square, hbm),
        (vector, vmem),
        (square, hbm),
        (vector, vmem),
        (vector, vmem),
        (vector, vmem),
        (shape(width, hidden), hbm),
        (shape(hidden), vmem),
        (shape(hidden, width), hbm),
        (vector, vmem),
    )
    return pl.pallas_call(
        spread_kernel,
        out_shape=tuple(out for out, _ in outs),
        in_specs=[pl.BlockSpec(memory_space=pltpu.HBM), vmem],
        out_specs=tuple(spec for _, spec in outs),
        scratch_shapes=[
            pltpu.VMEM((DEPTH, width, half), BF),
            pltpu.VMEM((DEPTH, width, half), F32),
            DMA((DEPTH,)),
            DMA((DEPTH,)),
            DMA((tables,)),
        ],
        compiler_params=pltpu.CompilerParams(vmem_limit_bytes=56 << 20),
        cost_estimate=pl.CostEstimate(flops=0, bytes_accessed=48 << 20, transcendentals=0),
    )(gath, table_grad)


def local(*args):
    layers = lax.axis_size("table")
    side = math.isqrt(lax.axis_size("dp") // 2)
    knowledge, expr_table, w_in = args[0], args[1], args[17]
    width, hidden = w_in.shape
    mixed, table_grad, total = layer(side, layers, args)
    total = total.reshape(-1, width, width // 2)
    return (mixed, *spread(total, table_grad, knowledge.shape[0], expr_table.shape[0], hidden))


def solution(mesh):
    rows = P(("dp", "table"))
    by_token = P(("dp", "table"), None)
    by_row = P(None, ("dp", "table"), None)
    in_specs = (by_row, P(), by_token, rows, rows, rows) + (P(),) * 15 + (by_token,)
    out_specs = (by_token, by_row) + (P(),) * 16
    return jax.shard_map(local, mesh=mesh, in_specs=in_specs, out_specs=out_specs, check_vma=False)
```

time: 707 us -> 203 us (0.29); the launches traced: 698 us -> 202 us
  waiting for transfers between devices: 481 us -> 0 us
  Pallas kernels: 0 us -> 201 us
  blocking collectives: 65.2 us -> 0 us
  local copies, waits for them, and re-layouts: 62.2 us -> 0.75 us
  matrix products: 54.2 us -> 0 us
  between operations: 15.4 us -> 0.7 us
  other arithmetic: 11.8 us -> 0 us
  starting transfers between devices: 9.12 us -> 0 us
    psum x1 -> x0, waiting for transfers between devices: 397 us -> none  [local(): lax.psum((w_in_grad, b_in_grad, w_out_grad, b_out_grad, norm2_gain_grad,...]
    pallas_call x0 -> x2, Pallas kernels: none -> 201 us  [the longest x1 184 us: layer(): pl.pallas_call(functools.partial(layer_kernel, (side, layers, cap, offset...]
    all_to_all x2 -> x0, waiting for transfers between devices: 84 us -> none  [the longest x1 84 us: local(): lax.all_to_all(picked.reshape(devices, slot_count, TABLES * model_width),...]
    dot_general x28 -> x0, matrix products: 54.2 us -> none  [the longest x1 6.3 us: local(): jnp.dot(act_low, w_out, preferred_element_type=jnp.float32)]
    psum x1 -> x0, blocking collectives: 50.9 us -> none  [local(): lax.psum((w_in_grad, b_in_grad, w_out_grad, b_out_grad, norm2_gain_grad,...]
    unnamed x151 -> x3, local copies, waits for them, and re-layouts: 26.8 us -> 0.75 us
    all_to_all x1 -> x0, blocking collectives: 14.3 us -> none  [local(): lax.all_to_all(outgoing, ('dp', 'table'), split_axis=0, concat_axis=0, ti...]
    convert_element_type x6 -> x0, local copies, waits for them, and re-layouts: 11.5 us -> none  [the longest x1 5.19 us: local(): picked = jnp.einsum('sr,krd->skd', row_hot, knowledge, preferred_element_...]
  transfers between devices with their start and end apart: 3 -> 0, of which waited for: 2 -> 0; matrix products, arithmetic and copies ran while one was open for 2% -> 0% of each run, Pallas kernels for 0% -> 0%
where the time goes in v1:
time: 203 us; the launch traced here: 202 us
  Pallas kernels  201 us (99%)
    pallas_call x1, Pallas kernels, layer(): pl.pallas_call(functools.partial(layer_kernel, (side, layers, cap, offset...  184 us
    pallas_call x1, Pallas kernels, spread(): pl.pallas_call(spread_kernel, out_shape=tuple((out for out, _ in outs)),...  17.4 us

profile of v1, /device:TPU:0, one launch (start us, length us, event | category | flops | bytes accessed | tf_op | source)
XLA Modules:
  0.0 202.5 jit_solution(8223722340006704639)
XLA Ops:
  0.7 183.6 %shard_map.349 = (bf16[256,768]{1,0:T(8,128)(2,1)}, f32[144,768]{1,0:T(8,128)}, bf16[25,2,2,4,48,384]{5,4,3,2,1,0:T(8,128)(2,1)}) custom-call(bf16[5,144,768]{2,1,0:T(8,128)(2,1)} %refs_0_.1, bf16[128,768]{1,0:T(8,128)(2,1)} %refs_1_.1, s32[1,256]{1,0:T(1,128)} %bitcast.5, s32[1,256]{1,0:T(1,128)} %bitcast.6, s32[1,256]{1,0:T(1,128)} %bitcast.7, s32[8]{0:T(128)} %refs_5_.1, ...), custom_call_target="tpu_custom_call" | custom-call | flops 10871635968 | bytes 41943040 | tf_op jit(solution)/shard_map/pallas_call | solution.py:749
  184.3 0.0 copy-start
  184.3 17.4 %shard_map.350 = (f32[5,144,768]{2,1,0:T(8,128)}, f32[128,768]{1,0:T(8,128)}, f32[768]{0:T(1024)}, f32[768]{0:T(1024)}, f32[768,768]{1,0:T(8,128)}, /*index=5*/f...) custom-call(bf16[25,768,384]{2,1,0:T(8,128)(2,1)} %bitcast.4, ...), custom_call_target="tpu_custom_call" | custom-call | bytes 50331648 | tf_op jit(solution)/shard_map/pallas_call | solution.py:866
  201.7 0.0 copy-done
  201.7 0.7 copy.41
Async XLA Ops:
  184.3 17.4 %copy-start = (bf16[256,768]{1,0:T(8,128)(2,1)S(1)}, bf16[256,768]{1,0:T(8,128)(2,1)}, u32[]{:S(2)}) copy-start(bf16[256,768]{1,0:T(8,128)(2,1)} %get-tuple-element.76) | copy-start | bytes 1179652

commit v2 on v1

--- a/solution.py
+++ b/solution.py
@@ -83,34 +83,41 @@
     def sent(self, src, send_sem):
         self.copy(src, src, send_sem, send_sem, self.other_core).wait_send()
 
+    def each_other(self, act):
+        layers = self.layers
+        for dz in sorted(range(layers), key=lambda d: -min(d, layers - d)):
+
+            def one(i, carry):
+                act(i * layers + dz)
+                return carry
+
+            lax.fori_loop(0 if dz else 1, self.count // layers, one, 0)
+
     def greet_all(self):
         bar = pltpu.get_barrier_semaphore()
 
-        def greet(step, carry):
+        def greet(step):
             to = self.flat(lax.rem(self.me + step, self.count))
             pl.semaphore_signal(bar, inc=1, device_id=to, device_id_type=MESH)
-            return carry
-
-        lax.fori_loop(1, self.count, greet, 0)
+
+        self.each_other(greet)
 
     def await_all(self):
         pl.semaphore_wait(pltpu.get_barrier_semaphore(), self.count - 1)
 
     def exchange_start(self, out, into, send_sem, recv_sems):
-        def start(step, carry):
+        def start(step):
             to = lax.rem(self.me + step, self.count)
             self.send(out.at[to], into.at[self.me], send_sem, recv_sems.at[step], self.flat(to))
-            return carry
-
-        lax.fori_loop(1, self.count, start, 0)
+
+        self.each_other(start)
 
     def exchange_wait(self, into, recv_sems):
-        def wait(step, carry):
+        def wait(step):
             origin = lax.rem(self.me + self.count - step, self.count)
             self.arrived(into.at[origin], recv_sems.at[step])
-            return carry
-
-        lax.fori_loop(1, self.count, wait, 0)
+
+        self.each_other(wait)
 
 
 class Reducer:
@@ -118,38 +125,36 @@
         self.p = place
         self.part, self.gath = part, gath
         self.core_buf, self.first_buf, self.z_buf, self.last_buf, self.z_sum, self.final = bufs
-        (
-            self.core_in,
-            self.first_in,
-            self.z_in,
-            self.last_in,
-            self.own_in,
-            self.z_back,
-            self.first_back,
-            self.core_back,
-        ) = recv
-        (
-            self.core_out,
-            self.first_out,
-            self.z_out,
-            self.last_out,
-            self.z_ret,
-            self.first_ret,
-            self.core_ret,
-        ) = sent
-        n = place.side
+        self.core_in, self.first_in, self.z_in, self.last_in, self.own_in = recv[:5]
+        self.z_back, self.first_back, self.core_back, self.last_back = recv[5:]
+        self.core_out, self.first_out, self.first_ret, self.core_ret = sent[:4]
+        self.z_out, self.z_ret, self.last_out, self.slim_out, self.slim_ret = sent[4:]
         layers = place.layers
-        self.stages = (
+        self.count = part.shape[0]
+        self.slims = SLIM // place.side * place.side
+        bind = functools.partial
+        steps, returns = range(1, layers - 1), range(1, layers)
+        self.wide_stages = (
             [self.first_sum]
-            + [functools.partial(self.z_step, s) for s in range(1, layers - 1)]
+            + [bind(self.z_step, s) for s in steps]
             + [self.z_final, self.last_sum]
-            + [functools.partial(self.z_return, s) for s in range(1, layers)]
-            + [self.core_return, self.finish]
+            + [bind(self.z_return, s) for s in returns[:-1]]
+            + [self.wide_z_return, self.core_return, self.finish]
         )
+        self.slim_stages = (
+            [self.slim_first_sum, self.slim_last_sum]
+            + [self.of_own(bind(self.z_step, s)) for s in steps]
+            + [self.slim_z_final]
+            + [self.of_own(bind(self.z_return, s)) for s in returns[:-1]]
+            + [self.slim_z_return, self.slim_last_return, self.slim_core_return, self.slim_finish]
+        )
 
     def axes(self, k):
         p = self.p
-        even = lax.rem(k, 2) == 0
+        if isinstance(k, int):
+            even = (k // p.side if k < self.slims else k) % 2 == 0
+        else:
+            even = lax.rem(jnp.where(k < self.slims, k // p.side, k), 2) == 0
         first = jnp.where(even, p.b, p.a)
         last = jnp.where(even, p.a, p.b)
 
@@ -162,6 +167,12 @@
             return q, p.at(jnp.where(even, q, p.a), jnp.where(even, p.b, q), p.core, p.z)
 
         return first, last, first_peer, last_peer
+
+    def before(self, position, m):
+        return lax.rem(position - m + self.p.side, self.p.side)
+
+    def of_own(self, act):
+        return lambda base: act(base + self.axes(base)[1])
 
     def core_send(self, k):
         p = self.p
@@ -190,7 +201,7 @@
                 to,
             )
 
-    def first_sum(self, k):
+    def add_first(self, k):
         p = self.p
         first, _, _, _ = self.axes(k)
         for m in range(1, p.side):
@@ -199,89 +210,102 @@
         for m in range(1, p.side):
             total = total + self.first_buf[k, m - 1].astype(F32)
         self.first_buf[k, 0] = total.astype(BF)
+
+    def first_sum(self, k):
+        self.add_first(k)
+        self.z_start(k)
+
+    def slim_first_sum(self, base):
+        p = self.p
+        for q in range(p.side):
+            self.add_first(base + q)
+        _, last, _, last_peer = self.axes(base)
+        for m in range(1, p.side):
+            q, to = last_peer(m)
+            p.send(
+                self.first_buf.at[base + q, 0],
+                self.z_buf.at[base + last, pl.ds(0, p.layers)],
+                self.slim_out,
+                self.last_in.at[base + q, m - 1],
+                to,
+            )
+
+    def slim_last_sum(self, base):
+        p = self.p
+        _, last, _, _ = self.axes(base)
+        own = base + last
+        total = self.first_buf[own, 0].astype(F32)
+        for m in range(1, p.side):
+            came = self.z_buf.at[base + self.before(last, m), pl.ds(0, p.layers)]
+            p.arrived(came, self.last_in.at[own, m - 1])
+            total = total + came[...].astype(F32)
+        self.first_buf[own, 0] = total.astype(BF)
+        self.z_start(own)
+
+    def z_send(self, k, src, slot, to):
+        self.p.send(src, self.z_buf.at[k, slot], self.z_out, self.z_in.at[k, slot], to)
+
+    def z_start(self, k):
+        p = self.p
         top = p.layers - 1
 
         @pl.when(p.z == 0)
         def _():
             for j in range(top, 0, -1):
-                slot = j if j > 1 else p.layers
-                p.send(
-                    self.first_buf.at[k, 0, j],
-                    self.z_buf.at[k, slot],
-                    self.z_out,
-                    self.z_in.at[k, slot],
-                    p.up,
-                )
+                self.z_send(k, self.first_buf.at[k, 0, j], j if j > 1 else p.layers, p.up)
 
         @pl.when(p.z == top)
         def _():
             for j in range(0, top):
-                p.send(
-                    self.first_buf.at[k, 0, j],
-                    self.z_buf.at[k, j],
-                    self.z_out,
-                    self.z_in.at[k, j],
-                    p.down,
-                )
-
-    def z_add(self, k, j):
-        self.p.arrived(self.z_buf.at[k, j], self.z_in.at[k, j])
-        self.z_buf[k, j] = (
-            self.z_buf[k, j].astype(F32) + self.first_buf[k, 0, j].astype(F32)
-        ).astype(BF)
+                self.z_send(k, self.first_buf.at[k, 0, j], j, p.down)
 
     def z_step(self, s, k):
         p = self.p
         top = p.layers - 1
 
+        def add(j):
+            p.arrived(self.z_buf.at[k, j], self.z_in.at[k, j])
+            self.z_buf[k, j] = (
+                self.z_buf[k, j].astype(F32) + self.first_buf[k, 0, j].astype(F32)
+            ).astype(BF)
+            return self.z_buf.at[k, j]
+
         @pl.when(p.z == s)
         def _():
             for j in range(top, s, -1):
-                self.z_add(k, j)
-                slot = j if j > s + 1 else p.layers
-                p.send(
-                    self.z_buf.at[k, j],
-                    self.z_buf.at[k, slot],
-                    self.z_out,
-                    self.z_in.at[k, slot],
-                    p.up,
-                )
+                self.z_send(k, add(j), j if j > s + 1 else p.layers, p.up)
 
         @pl.when(p.z == top - s)
         def _():
             for j in range(0, top - s):
-                self.z_add(k, j)
-                p.send(
-                    self.z_buf.at[k, j],
-                    self.z_buf.at[k, j],
-                    self.z_out,
-                    self.z_in.at[k, j],
-                    p.down,
-                )
-
-    def z_final(self, k):
+                self.z_send(k, add(j), j, p.down)
+
+    def z_total(self, k, into):
         p = self.p
         top = p.layers - 1
-        _, _, _, last_peer = self.axes(k)
 
         def arrival(slot):
             p.arrived(self.z_buf.at[k, slot], self.z_in.at[k, slot])
             return self.z_buf[k, slot].astype(F32)
 
-        own = self.first_buf[k, 0, p.z].astype(F32)
+        mine = self.first_buf[k, 0, p.z].astype(F32)
 
         @pl.when(p.z == 0)
         def _():
-            self.z_sum[k] = (own + arrival(0)).astype(BF)
+            into[k] = (mine + arrival(0)).astype(BF)
 
         @pl.when(p.z == top)
         def _():
-            self.z_sum[k] = (own + arrival(p.layers)).astype(BF)
+            into[k] = (mine + arrival(p.layers)).astype(BF)
 
         @pl.when((p.z > 0) & (p.z < top))
         def _():
-            self.z_sum[k] = (own + arrival(p.layers) + arrival(p.z)).astype(BF)
-
+            into[k] = (mine + arrival(p.layers) + arrival(p.z)).astype(BF)
+
+    def z_final(self, k):
+        p = self.p
+        _, _, _, last_peer = self.axes(k)
+        self.z_total(k, self.z_sum)
         for m in range(1, p.side):
             _, to = last_peer(m)
             p.send(
@@ -292,14 +316,19 @@
                 to,
             )
 
+    def slim_z_final(self, base):
+        own = base + self.axes(base)[1]
+        self.z_total(own, self.final)
+        self.z_return_start(own)
+
     def last_sum(self, k):
         p = self.p
-        first, last, _, _ = self.axes(k)
+        _, last, _, _ = self.axes(k)
         for m in range(1, p.side):
             p.arrived(self.last_buf.at[k, m - 1], self.last_in.at[k, m - 1])
         total = None
         for q in range(p.side):
-            m = lax.rem(last - q + p.side, p.side)
+            m = self.before(last, q)
             term = jnp.where(
                 m == 0,
                 self.z_sum[k].astype(F32),
@@ -307,84 +336,125 @@
             )
             total = term if total is None else total + term
         self.final[k] = total.astype(BF)
-        own = self.final.at[k]
-        there = self.gath.at[k, p.core, first, p.z]
-        pltpu.make_async_copy(own, there, self.own_in.at[k]).start()
+        self.z_return_start(k)
+
+    def own_copy(self, k):
+        p = self.p
+        there = self.gath.at[k, p.core, self.axes(k)[0], p.z]
+        return there, pltpu.make_async_copy(self.final.at[k], there, self.own_in.at[k])
+
+    def z_return_start(self, k):
+        p = self.p
+        there, copy = self.own_copy(k)
+        copy.start()
 
         @pl.when(p.z < p.layers - 1)
         def _():
-            p.send(own, there, self.z_ret, self.z_back.at[k, p.z], p.up)
+            p.send(self.final.at[k], there, self.z_ret, self.z_back.at[k, p.z], p.up)
 
         @pl.when(p.z > 0)
         def _():
-            p.send(own, there, self.z_ret, self.z_back.at[k, p.z], p.down)
+            p.send(self.final.at[k], there, self.z_ret, self.z_back.at[k, p.z], p.down)
 
     def z_return(self, s, k):
         p = self.p
-        first, _, first_peer, _ = self.axes(k)
+        first, _, _, _ = self.axes(k)
         top = p.layers - 1
 
-        @pl.when(p.z >= s)
-        def _():
-            j = jnp.maximum(p.z - s, 0)
+        def forward(j, ahead, to):
             shard = self.gath.at[k, p.core, first, j]
             p.arrived(shard, self.z_back.at[k, j])
 
-            @pl.when(p.z < top)
+            @pl.when(ahead)
             def _():
-                p.send(shard, shard, self.z_ret, self.z_back.at[k, j], p.up)
+                p.send(shard, shard, self.z_ret, self.z_back.at[k, j], to)
+
+        @pl.when(p.z >= s)
+        def _():
+            forward(jnp.maximum(p.z - s, 0), p.z < top, p.up)
 
         @pl.when(p.z <= top - s)
         def _():
-            j = jnp.minimum(p.z + s, top)
-            shard = self.gath.at[k, p.core, first, j]
-            p.arrived(shard, self.z_back.at[k, j])
-
-            @pl.when(p.z > 0)
-            def _():
-                p.send(shard, shard, self.z_ret, self.z_back.at[k, j], p.down)
+            forward(jnp.minimum(p.z + s, top), p.z > 0, p.down)
 
         if s == top:
-            own = self.final.at[k]
-            pltpu.make_async_copy(
-                own, self.gath.at[k, p.core, first, p.z], self.own_in.at[k]
-            ).wait()
-            mine = self.gath.at[k, p.core, first]
-            for m in range(1, p.side):
-                _, to = first_peer(m)
-                p.send(mine, mine, self.first_ret, self.first_back.at[k, m - 1], to)
+            self.own_copy(k)[1].wait()
+
+    def send_first(self, k, chunks):
+        p = self.p
+        first, _, first_peer, _ = self.axes(k)
+        mine = self.gath.at[chunks, p.core, first]
+        for m in range(1, p.side):
+            p.send(mine, mine, self.first_ret, self.first_back.at[k, m - 1], first_peer(m)[1])
+
+    def send_core(self, k, chunks):
+        p = self.p
+        first, _, _, _ = self.axes(k)
+        for m in range(1, p.side):
+            came = self.gath.at[chunks, p.core, self.before(first, m)]
+            p.arrived(came, self.first_back.at[k, m - 1])
+        mine = self.gath.at[chunks, p.core]
+        p.send(mine, mine, self.core_ret, self.core_back.at[k], p.other_core)
+
+    def wide_z_return(self, k):
+        self.z_return(self.p.layers - 1, k)
+        self.send_first(k, k)
 
     def core_return(self, k):
-        p = self.p
-        first, _, _, _ = self.axes(k)
-        for m in range(1, p.side):
-            q = lax.rem(first - m + p.side, p.side)
-            p.arrived(self.gath.at[k, p.core, q], self.first_back.at[k, m - 1])
-        mine = self.gath.at[k, p.core]
-        p.send(mine, mine, self.core_ret, self.core_back.at[k], p.other_core)
+        self.send_core(k, k)
 
     def finish(self, k):
-        p = self.p
-        p.arrived(self.gath.at[k, 1 - p.core], self.core_back.at[k])
+        self.p.arrived(self.gath.at[k, 1 - self.p.core], self.core_back.at[k])
+
+    def slim_z_return(self, base):
+        p = self.p
+        first, last, _, last_peer = self.axes(base)
+        own = base + last
+        self.z_return(p.layers - 1, own)
+        mine = self.gath.at[own, p.core, first]
+        for m in range(1, p.side):
+            p.send(mine, mine, self.slim_ret, self.last_back.at[own, m - 1], last_peer(m)[1])
+
+    def slim_last_return(self, base):
+        p = self.p
+        first, last, _, _ = self.axes(base)
+        for m in range(1, p.side):
+            k = base + self.before(last, m)
+            p.arrived(self.gath.at[k, p.core, first], self.last_back.at[k, m - 1])
+        self.send_first(base, pl.ds(base, p.side))
+
+    def slim_core_return(self, base):
+        self.send_core(base, pl.ds(base, self.p.side))
+
+    def slim_finish(self, base):
+        unit = self.gath.at[pl.ds(base, self.p.side), 1 - self.p.core]
+        self.p.arrived(unit, self.core_back.at[base])
 
     def drain(self):
         p = self.p
+        units = self.slims // p.side
+        wides = self.count - self.slims
+        chains = pl.ds(0, wides + units)
         p.sent(self.core_buf, self.core_out)
         p.sent(self.first_buf, self.first_out)
-        p.sent(self.z_buf.at[:, pl.ds(0, p.layers - 1)], self.z_out)
-        p.sent(self.last_buf, self.last_out)
-        middle = (p.z > 0) & (p.z < p.layers - 1)
-
-        @pl.when(middle)
-        def _():
-            p.sent(self.z_buf, self.z_ret)
-
-        @pl.when(jnp.logical_not(middle))
-        def _():
-            p.sent(self.z_buf.at[:, pl.ds(0, 1)], self.z_ret)
-
         p.sent(self.first_buf, self.first_ret)
         p.sent(self.core_buf, self.core_ret)
+        p.sent(self.z_buf.at[chains, pl.ds(0, p.layers - 1)], self.z_out)
+        middle = (p.z > 0) & (p.z < p.layers - 1)
+
+        @pl.when(middle)
+        def _():
+            p.sent(self.z_buf.at[chains], self.z_ret)
+
+        @pl.when(jnp.logical_not(middle))
+        def _():
+            p.sent(self.z_buf.at[chains, pl.ds(0, 1)], self.z_ret)
+
+        if wides:
+            p.sent(self.last_buf.at[pl.ds(0, wides)], self.last_out)
+        if units:
+            p.sent(self.first_buf.at[pl.ds(0, units)], self.slim_out)
+            p.sent(self.first_buf.at[pl.ds(0, units)], self.slim_ret)
 
 
 def reducer_scratch(count, side, layers, rows, wide):
@@ -405,8 +475,9 @@
         DMA((count, layers)),
         DMA((count, side - 1)),
         DMA((count,)),
+        DMA((count, side - 1)),
     ]
-    return bufs, recv, [DMA(())] * 7
+    return bufs, recv, [DMA(())] * 9
 
 
 def layer_kernel(cfg, *refs):
@@ -427,7 +498,7 @@
     (embedded_v, attn_in_v, query_v, key_v, value_v, probs_v, context_v) = take(7)
     (hidden1_v, ffn_in_v, grad_ffn_v, acc_v, gn2_v, biases_v) = take(6)
     (part,) = take(1)
-    bufs, recv, sent = take(6), take(8), take(7)
+    bufs, recv, sent = take(6), take(9), take(9)
     assert not refs
 
     side, layers, cap, offsets = cfg
@@ -562,10 +633,43 @@
     gn2_v[...] = jnp.zeros_like(gn2_v)
     biases_v[...] = jnp.zeros_like(biases_v)
     shard = part.shape[1:]
+    plans = []
+    for stages, lags in zip((red.wide_stages, red.slim_stages), offsets):
+        reach = [0]
+        for lag in lags:
+            reach.append(reach[-1] + lag)
+        assert len(reach) == len(stages)
+        plans.append(list(zip(stages, reach)))
+    longest = max(plan[-1][1] for plan in plans)
+
+    def step(i):
+        for slim, plan in enumerate(plans):
+            for stage, lag in sorted(plan, key=lambda entry: -entry[1]):
+                k = i - lag
+                ahead = side - 1 if slim else 0
+                low, high = (0, red.slims) if slim else (red.slims, count)
+                if isinstance(k, int):
+                    if low <= k < high and (not slim or k % side == ahead):
+                        stage(k - ahead)
+                elif low < high:
+                    now = (k >= low) & (k < high)
+                    if slim:
+                        now = now & (lax.rem(k, side) == ahead)
+
+                    @pl.when(now)
+                    def _():
+                        stage(k - ahead)
 
     def put(k, values):
         part[k] = values.reshape(shard).astype(BF)
         red.core_send(k)
+
+    done = [0]
+
+    def pipe(where):
+        for _ in range(PIPE.get(where, 0)):
+            step(done[0])
+            done[0] += 1
 
     def put_bias(row, values):
         biases_v[pl.ds(2 * row, 1), :] = values[:, :half]
@@ -584,6 +688,9 @@
         )
         grad_pre = dot(grad_ffn_v[...], wout[...], 1, 1) * slope
         grad_pre = grad_pre.astype(BF)
+        if j:
+            for q in range(4):
+                red.core_sum(4 * (j - 1) + q)
         for h in range(2):
             put(4 * j + h, dot(act, grad_ffn_v[:, h * half : (h + 1) * half], 0, 0))
         for h in range(2):
@@ -594,9 +701,7 @@
             loads[10 + 2 * j].start()
             loads[11 + 2 * j].start()
         put_bias(j, column_sum(grad_pre.astype(F32)))
-        if j:
-            for q in range(4):
-                red.core_sum(4 * (j - 1) + q)
+        pipe(f'ffn{j}')
     at = 4 * blocks
     mixed[...] = (
         (hidden1_v[...] + acc_v[...] + b_out[...].reshape(1, width)) * live
@@ -613,6 +718,7 @@
     put_bias(blocks + 3, column_sum(grad_attn.astype(F32)))
     for h in range(2):
         put(at + h, dot(context_v[...], grad_attn[:, h * half : (h + 1) * half], 0, 0))
+    pipe('out')
     gctx_v = ffn_in_v
     gctx_v[...] = dot(grad_attn, wo_v[...], 1, 1).astype(BF)
     gq_v, gk_v, gv_v = query_v, key_v, value_v
@@ -629,6 +735,7 @@
         gq_v[:, lanes] = grad_query.astype(BF)
         gk_v[:, lanes] = grad_key.astype(BF)
         gv_v[:, lanes] = dot(probs.astype(BF), grads, 0, 0).astype(BF)
+        pipe(f'pair{pair}')
     for q in range(2):
         red.core_sum(at + q)
     at += 2
@@ -636,6 +743,7 @@
         for h in range(2):
             put(at + h, dot(attn_in_v[...], grad[:, h * half : (h + 1) * half], 0, 0))
         at += 2
+        pipe(f'grad{at}')
     put_bias(blocks + 4, column_sum(gq_v[...].astype(F32)))
     put_bias(blocks + 5, column_sum(gv_v[...].astype(F32)))
     grad_normed1 = dot(gq_v[...], wq_v[...], 1, 1)
@@ -659,26 +767,16 @@
         jnp.concatenate([expr_grad[:, :half], expr_grad[:, half:], biases_v[...], filler], axis=0),
     )
     place.exchange_start(back_out, back_in, back_sent, ids_sem)
+    pipe('back')
     back_in[place.me] = back_out[place.me]
     for k in range(at - 6, at + 1):
         red.core_sum(k)
 
-    reach = [0]
-    for offset in offsets:
-        reach.append(reach[-1] + offset)
-    assert len(reach) == len(red.stages)
-
-    def step(i, carry):
-        for stage, lag in reversed(list(zip(red.stages, reach))):
-            k = i - lag
-
-            @pl.when((k >= 0) & (k < count))
-            def _():
-                stage(k)
-
+    def later(i, carry):
+        step(i)
         return carry
 
-    lax.fori_loop(0, count + reach[-1], step, 0)
+    lax.fori_loop(done[0], count + longest, later, 0)
     place.exchange_wait(back_in, ids_sem)
     table_grad[...] = dot(row_hot_v[...], back_in[...].reshape(slots, width), 0, 0)
     place.sent(ids_out.at[pl.ds(0, devices - 1)], ids_sent)
@@ -770,9 +868,11 @@
     )
 
 
-OFFSETS = [2, 2, 2, 2, 2, 2, 2, 3, 1]
+OFFSETS = ([2, 1, 1, 3, 2, 2, 1, 4, 4], [3, 2, 2, 1, 2, 1, 0, 3, 4, 3])
+SLIM = 10
+PIPE = {"ffn2": 2, "ffn3": 2, "pair2": 1, "pair4": 1, "grad20": 1, "grad22": 1, "grad24": 1, "back": 2}
 VMEM_BYTES = 62 << 20
-DEPTH = 4
+DEPTH = 8
 
 
 def spread_kernel(gath, table_grad, *refs):

time: 203 us -> 192 us (0.946)
  Pallas kernels: 201 us -> 190 us
    pallas_call x1, Pallas kernels: 184 us -> 172 us  [layer(): pl.pallas_call(functools.partial(layer_kernel, (side, layers, cap, offset...]
where the time goes in v2:
time: 192 us; the launch traced here: 191 us
  Pallas kernels  190 us (99%)
    pallas_call x1, Pallas kernels, layer(): pl.pallas_call(functools.partial(layer_kernel, (side, layers, cap, offset...  172 us
    pallas_call x1, Pallas kernels, spread(): pl.pallas_call(spread_kernel, out_shape=tuple((out for out, _ in outs)),...  17.4 us

profile of v2, /device:TPU:0, one launch (start us, length us, event | category | flops | bytes accessed | tf_op | source)
XLA Modules:
  0.0 191.0 jit_solution(11626073396755473078)
XLA Ops:
  0.7 172.2 %shard_map.349 = (bf16[256,768]{1,0:T(8,128)(2,1)}, f32[144,768]{1,0:T(8,128)}, bf16[25,2,2,4,48,384]{5,4,3,2,1,0:T(8,128)(2,1)}) custom-call(bf16[5,144,768]{2,1,0:T(8,128)(2,1)} %refs_0_.1, bf16[128,768]{1,0:T(8,128)(2,1)} %refs_1_.1, s32[1,256]{1,0:T(1,128)} %bitcast.5, s32[1,256]{1,0:T(1,128)} %bitcast.6, s32[1,256]{1,0:T(1,128)} %bitcast.7, s32[8]{0:T(128)} %refs_5_.1, ...), custom_call_target="tpu_custom_call" | custom-call | flops 10871635968 | bytes 41943040 | tf_op jit(solution)/shard_map/pallas_call | solution.py:847
  172.8 0.0 copy-start
  172.8 17.4 %shard_map.350 = (f32[5,144,768]{2,1,0:T(8,128)}, f32[128,768]{1,0:T(8,128)}, f32[768]{0:T(1024)}, f32[768]{0:T(1024)}, f32[768,768]{1,0:T(8,128)}, /*index=5*/f...) custom-call(bf16[25,768,384]{2,1,0:T(8,128)(2,1)} %bitcast.4, ...), custom_call_target="tpu_custom_call" | custom-call | bytes 50331648 | tf_op jit(solution)/shard_map/pallas_call | solution.py:966
  190.2 0.0 copy-done
  190.3 0.7 copy.41
Async XLA Ops:
  172.8 17.4 %copy-start = (bf16[256,768]{1,0:T(8,128)(2,1)S(1)}, bf16[256,768]{1,0:T(8,128)(2,1)}, u32[]{:S(2)}) copy-start(bf16[256,768]{1,0:T(8,128)(2,1)} %get-tuple-element.76) | copy-start | bytes 1179652

commit v3 on v2

--- a/solution.py
+++ b/solution.py
@@ -497,7 +497,7 @@
     ids_sem, rows_sem, ids_sent, rows_sent, back_sent = take(5)
     (embedded_v, attn_in_v, query_v, key_v, value_v, probs_v, context_v) = take(7)
     (hidden1_v, ffn_in_v, grad_ffn_v, acc_v, gn2_v, biases_v) = take(6)
-    (part,) = take(1)
+    part, table_v, mixed_v, result_sems = take(4)
     bufs, recv, sent = take(6), take(9), take(9)
     assert not refs
 
@@ -703,7 +703,7 @@
         put_bias(j, column_sum(grad_pre.astype(F32)))
         pipe(f'ffn{j}')
     at = 4 * blocks
-    mixed[...] = (
+    mixed_v[...] = (
         (hidden1_v[...] + acc_v[...] + b_out[...].reshape(1, width)) * live
     ).astype(BF)
     put_bias(blocks, column_sum(grad_ffn_v[...].astype(F32)))
@@ -776,9 +776,19 @@
         step(i)
         return carry
 
-    lax.fori_loop(done[0], count + longest, later, 0)
+    middle = min(done[0] + MIDDLE, count + longest)
+    lax.fori_loop(done[0], middle, later, 0)
     place.exchange_wait(back_in, ids_sem)
-    table_grad[...] = dot(row_hot_v[...], back_in[...].reshape(slots, width), 0, 0)
+    table_v[...] = dot(row_hot_v[...], back_in[...].reshape(slots, width), 0, 0)
+    results = [
+        pltpu.make_async_copy(table_v, table_grad, result_sems.at[0]),
+        pltpu.make_async_copy(mixed_v, mixed, result_sems.at[1]),
+    ]
+    for result in results:
+        result.start()
+    lax.fori_loop(middle, count + longest, later, 0)
+    for result in results:
+        result.wait()
     place.sent(ids_out.at[pl.ds(0, devices - 1)], ids_sent)
     place.sent(back_out.at[pl.ds(0, devices - 1)], back_sent)
     red.drain()
@@ -836,6 +846,9 @@
         wide(F32),
         pltpu.VMEM((8 * ((2 * (blocks + 8) + 7) // 8), half), F32),
         pltpu.VMEM(whole, BF),
+        pltpu.VMEM((table_rows, width), F32),
+        wide(BF),
+        DMA((2,)),
     ]
     vmem = pl.BlockSpec(memory_space=pltpu.VMEM)
     hbm = pl.BlockSpec(memory_space=pl.ANY)
@@ -852,7 +865,7 @@
             jax.ShapeDtypeStruct(whole, BF),
         ),
         in_specs=specs,
-        out_specs=(vmem, vmem, hbm),
+        out_specs=(hbm, hbm, hbm),
         scratch_shapes=scratch + bufs + recv + sent,
         compiler_params=pltpu.CompilerParams(
             collective_id=1, has_side_effects=True, vmem_limit_bytes=VMEM_BYTES
@@ -871,14 +884,15 @@
 OFFSETS = ([2, 1, 1, 3, 2, 2, 1, 4, 4], [3, 2, 2, 1, 2, 1, 0, 3, 4, 3])
 SLIM = 10
 PIPE = {"ffn2": 2, "ffn3": 2, "pair2": 1, "pair4": 1, "grad20": 1, "grad22": 1, "grad24": 1, "back": 2}
+MIDDLE = 14
 VMEM_BYTES = 62 << 20
 DEPTH = 8
 
 
-def spread_kernel(gath, table_grad, *refs):
-    (know_out, expr_out, gain1_out, bias1_out, wq_out, bq_out, wk_out, wv_out, bv_out) = refs[:9]
-    (wo_out, bo1_out, gain2_out, bias2_out, win_out, bin_out, wout_out, bout_out) = refs[9:17]
-    narrow, broad, in_sems, out_sems, know_sems = refs[17:]
+def spread_kernel(gath, table_grad, mixed, *refs):
+    (mixed_out, know_out, expr_out, gain1_out, bias1_out, wq_out, bq_out, wk_out, wv_out) = refs[:9]
+    (bv_out, wo_out, bo1_out, gain2_out, bias2_out, win_out, bin_out, wout_out, bout_out) = refs[9:18]
+    narrow, broad, small, table_v, in_sems, out_sems, know_sems, more_sems = refs[18:]
     count, width, half = gath.shape
     blocks = win_out.shape[1] // width
     places = []
@@ -891,7 +905,8 @@
     for out in (wo_out, wq_out, wk_out, wv_out):
         for h in range(2):
             places.append(out.at[:, pl.ds(h * half, half)])
-    assert len(places) == count - 1
+    last = count - 1
+    assert len(places) == last
 
     def fetch(k):
         return pltpu.make_async_copy(gath.at[k], narrow.at[k % DEPTH], in_sems.at[k % DEPTH])
@@ -901,27 +916,38 @@
 
     for k in range(DEPTH - 1):
         fetch(k).start()
+    more = [
+        pltpu.make_async_copy(gath.at[last, pl.ds(0, small.shape[0])], small, more_sems.at[0]),
+        pltpu.make_async_copy(table_grad, table_v, more_sems.at[1]),
+        pltpu.make_async_copy(mixed, mixed_out, more_sems.at[2]),
+    ]
+    for copy in more:
+        copy.start()
     knows = [
-        pltpu.make_async_copy(table_grad, know_out.at[i], know_sems.at[i])
+        pltpu.make_async_copy(table_v, know_out.at[i], know_sems.at[i])
         for i in range(know_out.shape[0])
     ]
-    for know in knows:
-        know.start()
-    for k in range(count):
-        if k + DEPTH - 1 < count:
-            fetch(k + DEPTH - 1).start()
+
+    def convert(k):
         fetch(k).wait()
-        if k == count - 1:
-            break
         if k >= DEPTH:
             store(k - DEPTH).wait()
         broad[k % DEPTH] = narrow[k % DEPTH].astype(F32)
         store(k).start()
-    small = narrow.at[(count - 1) % DEPTH]
+        if k + DEPTH < last:
+            fetch(k + DEPTH).start()
+
+    fetch(DEPTH - 1).start()
+    for k in range(DEPTH):
+        convert(k)
+    more[1].wait()
+    for know in knows:
+        know.start()
+    more[0].wait()
     bins = expr_out.shape[0]
     expr_out[:, :half] = small[pl.ds(0, bins), :].astype(F32)
     expr_out[:, half:] = small[pl.ds(bins, bins), :].astype(F32)
-    biases = small[pl.ds(2 * bins, 8 * ((2 * (blocks + 8) + 7) // 8)), :].astype(F32)
+    biases = small[pl.ds(2 * bins, small.shape[0] - 2 * bins), :].astype(F32)
 
     def bias(i):
         return jnp.concatenate([biases[2 * i : 2 * i + 1], biases[2 * i + 1 : 2 * i + 2]], axis=1)[0]
@@ -932,19 +958,23 @@
         (bout_out, gain2_out, bias2_out, bo1_out, bq_out, bv_out, gain1_out, bias1_out)
     ):
         out[...] = bias(blocks + i)
-    for k in range(max(0, count - 1 - DEPTH), count - 1):
+    for k in range(DEPTH, last):
+        convert(k)
+    for k in range(last - DEPTH, last):
         store(k).wait()
     for know in knows:
         know.wait()
-
-
-def spread(gath, table_grad, tables, bins, hidden):
+    more[2].wait()
+
+
+def spread(gath, table_grad, mixed, tables, bins, hidden):
     count, width, half = gath.shape
     shape = lambda *dims: jax.ShapeDtypeStruct(dims, F32)
     vector, square = shape(width), shape(width, width)
     vmem = pl.BlockSpec(memory_space=pltpu.VMEM)
     hbm = pl.BlockSpec(memory_space=pl.ANY)
     outs = (
+        (jax.ShapeDtypeStruct(mixed.shape, mixed.dtype), hbm),
         (shape(tables, *table_grad.shape), hbm),
         (shape(bins, width), vmem),
         (vector, vmem),
@@ -966,18 +996,21 @@
     return pl.pallas_call(
         spread_kernel,
         out_shape=tuple(out for out, _ in outs),
-        in_specs=[pl.BlockSpec(memory_space=pltpu.HBM), vmem],
+        in_specs=[pl.BlockSpec(memory_space=pltpu.HBM)] * 3,
         out_specs=tuple(spec for _, spec in outs),
         scratch_shapes=[
             pltpu.VMEM((DEPTH, width, half), BF),
             pltpu.VMEM((DEPTH, width, half), F32),
+            pltpu.VMEM((2 * bins + 16 * ((2 * (hidden // width + 8) + 15) // 16), half), BF),
+            pltpu.VMEM(table_grad.shape, F32),
             DMA((DEPTH,)),
             DMA((DEPTH,)),
             DMA((tables,)),
+            DMA((3,)),
         ],
-        compiler_params=pltpu.CompilerParams(vmem_limit_bytes=56 << 20),
+        compiler_params=pltpu.CompilerParams(vmem_limit_bytes=60 << 20),
         cost_estimate=pl.CostEstimate(flops=0, bytes_accessed=48 << 20, transcendentals=0),
-    )(gath, table_grad)
+    )(gath, table_grad, mixed)
 
 
 def local(*args):
@@ -987,7 +1020,7 @@
     width, hidden = w_in.shape
     mixed, table_grad, total = layer(side, layers, args)
     total = total.reshape(-1, width, width // 2)
-    return (mixed, *spread(total, table_grad, knowledge.shape[0], expr_table.shape[0], hidden))
+    return spread(total, table_grad, mixed, knowledge.shape[0], expr_table.shape[0], hidden)
 
 
 def solution(mesh):

time: 192 us -> 188 us (0.979)
  Pallas kernels: 190 us -> 187 us
where the time goes in v3:
time: 188 us
  Pallas kernels  187 us (99%)
    pallas_call x1, Pallas kernels, layer(): pl.pallas_call(functools.partial(layer_kernel, (side, layers, cap, offset...  171 us
    pallas_call x1, Pallas kernels, spread(): pl.pallas_call(spread_kernel, out_shape=tuple((out for out, _ in outs)),...  15.5 us

profile of v3, /device:TPU:0, one launch (start us, length us, event | category | flops | bytes accessed | tf_op | source)
XLA Modules:
  0.0 187.8 jit_solution(13883714729367246977)
XLA Ops:
  0.7 171.4 %shard_map.349 = (bf16[256,768]{1,0:T(8,128)(2,1)}, f32[144,768]{1,0:T(8,128)}, bf16[25,2,2,4,48,384]{5,4,3,2,1,0:T(8,128)(2,1)}) custom-call(bf16[5,144,768]{2,1,0:T(8,128)(2,1)} %refs_0_.1, bf16[128,768]{1,0:T(8,128)(2,1)} %refs_1_.1, s32[1,256]{1,0:T(1,128)} %bitcast.5, s32[1,256]{1,0:T(1,128)} %bitcast.6, s32[1,256]{1,0:T(1,128)} %bitcast.7, s32[8]{0:T(128)} %refs_5_.1, ...), custom_call_target="tpu_custom_call" | custom-call | flops 10871635968 | bytes 41943040 | tf_op jit(solution)/shard_map/pallas_call | solution.py:860
  172.1 15.5 %shard_map.350 = (bf16[256,768]{1,0:T(8,128)(2,1)}, f32[5,144,768]{2,1,0:T(8,128)}, f32[128,768]{1,0:T(8,128)}, f32[768]{0:T(1024)}, f32[768]{0:T(1024)}, /*inde...) custom-call(bf16[25,768,384]{2,1,0:T(8,128)(2,1)} %bitcast.4, ...), custom_call_target="tpu_custom_call" | custom-call | bytes 50331648 | tf_op jit(solution)/shard_map/pallas_call | solution.py:996

commit v4 on v3

--- a/solution.py
+++ b/solution.py
@@ -83,9 +83,13 @@
     def sent(self, src, send_sem):
         self.copy(src, src, send_sem, send_sem, self.other_core).wait_send()
 
-    def each_other(self, act):
+    def far_first(self):
         layers = self.layers
-        for dz in sorted(range(layers), key=lambda d: -min(d, layers - d)):
+        return sorted(range(layers), key=lambda d: -min(d, layers - d))
+
+    def each_other(self, act, offsets=None):
+        layers = self.layers
+        for dz in self.far_first() if offsets is None else offsets:
 
             def one(i, carry):
                 act(i * layers + dz)
@@ -105,12 +109,12 @@
     def await_all(self):
         pl.semaphore_wait(pltpu.get_barrier_semaphore(), self.count - 1)
 
-    def exchange_start(self, out, into, send_sem, recv_sems):
+    def exchange_start(self, out, into, send_sem, recv_sems, offsets=None):
         def start(step):
             to = lax.rem(self.me + step, self.count)
             self.send(out.at[to], into.at[self.me], send_sem, recv_sems.at[step], self.flat(to))
 
-        self.each_other(start)
+        self.each_other(start, offsets)
 
     def exchange_wait(self, into, recv_sems):
         def wait(step):
@@ -766,7 +770,6 @@
         at,
         jnp.concatenate([expr_grad[:, :half], expr_grad[:, half:], biases_v[...], filler], axis=0),
     )
-    place.exchange_start(back_out, back_in, back_sent, ids_sem)
     pipe('back')
     back_in[place.me] = back_out[place.me]
     for k in range(at - 6, at + 1):
@@ -776,8 +779,16 @@
         step(i)
         return carry
 
-    middle = min(done[0] + MIDDLE, count + longest)
+    total = count + longest
+    middle = min(max(MIDDLE, done[0]), total)
     lax.fori_loop(done[0], middle, later, 0)
+    for dz in place.far_first():
+        place.exchange_start(back_out, back_in, back_sent, ids_sem, [dz])
+        if middle < total:
+            step(middle)
+            middle += 1
+    end = min(middle + SETTLE, total)
+    lax.fori_loop(middle, end, later, 0)
     place.exchange_wait(back_in, ids_sem)
     table_v[...] = dot(row_hot_v[...], back_in[...].reshape(slots, width), 0, 0)
     results = [
@@ -786,7 +797,7 @@
     ]
     for result in results:
         result.start()
-    lax.fori_loop(middle, count + longest, later, 0)
+    lax.fori_loop(end, total, later, 0)
     for result in results:
         result.wait()
     place.sent(ids_out.at[pl.ds(0, devices - 1)], ids_sent)
@@ -881,10 +892,11 @@
     )
 
 
-OFFSETS = ([2, 1, 1, 3, 2, 2, 1, 4, 4], [3, 2, 2, 1, 2, 1, 0, 3, 4, 3])
+OFFSETS = ([2, 1, 1, 3, 2, 2, 1, 6, 6], [4, 2, 2, 1, 2, 1, 0, 3, 7, 2])
 SLIM = 10
-PIPE = {"ffn2": 2, "ffn3": 2, "pair2": 1, "pair4": 1, "grad20": 1, "grad22": 1, "grad24": 1, "back": 2}
-MIDDLE = 14
+PIPE = {"ffn2": 2, "ffn3": 2, "pair2": 2, "pair4": 1, "grad20": 1, "grad22": 1, "grad24": 2, "back": 1, "pair5": 1}
+MIDDLE = 35
+SETTLE = 8
 VMEM_BYTES = 62 << 20
 DEPTH = 8
 

time: 188 us -> 182 us (0.968)
  Pallas kernels: 187 us -> 181 us
    pallas_call x1, Pallas kernels: 171 us -> 166 us  [layer(): pl.pallas_call(functools.partial(layer_kernel, (side, layers, cap, offset...]
where the time goes in v4:
time: 182 us
  Pallas kernels  181 us (99%)
    pallas_call x1, Pallas kernels, layer(): pl.pallas_call(functools.partial(layer_kernel, (side, layers, cap, offset...  166 us
    pallas_call x1, Pallas kernels, spread(): pl.pallas_call(spread_kernel, out_shape=tuple((out for out, _ in outs)),...  15.5 us

profile of v4, /device:TPU:0, one launch (start us, length us, event | category | flops | bytes accessed | tf_op | source)
XLA Modules:
  0.0 182.2 jit_solution(15548729793782252278)
XLA Ops:
  0.7 165.9 %shard_map.349 = (bf16[256,768]{1,0:T(8,128)(2,1)}, f32[144,768]{1,0:T(8,128)}, bf16[25,2,2,4,48,384]{5,4,3,2,1,0:T(8,128)(2,1)}) custom-call(bf16[5,144,768]{2,1,0:T(8,128)(2,1)} %refs_0_.1, bf16[128,768]{1,0:T(8,128)(2,1)} %refs_1_.1, s32[1,256]{1,0:T(1,128)} %bitcast.5, s32[1,256]{1,0:T(1,128)} %bitcast.6, s32[1,256]{1,0:T(1,128)} %bitcast.7, s32[8]{0:T(128)} %refs_5_.1, ...), custom_call_target="tpu_custom_call" | custom-call | flops 10871635968 | bytes 41943040 | tf_op jit(solution)/shard_map/pallas_call | solution.py:871
  166.6 15.5 %shard_map.350 = (bf16[256,768]{1,0:T(8,128)(2,1)}, f32[5,144,768]{2,1,0:T(8,128)}, f32[128,768]{1,0:T(8,128)}, f32[768]{0:T(1024)}, f32[768]{0:T(1024)}, /*inde...) custom-call(bf16[25,768,384]{2,1,0:T(8,128)(2,1)} %bitcast.4, ...), custom_call_target="tpu_custom_call" | custom-call | bytes 50331648 | tf_op jit(solution)/shard_map/pallas_call | solution.py:1008

commit v5 on v4

--- a/solution.py
+++ b/solution.py
@@ -516,6 +516,8 @@
     count = part.shape[0]
     slots = devices * cap
 
+    place.greet_all()
+
     loads = [
         (knowledge, know_v),
         (w_query, wq_v),
@@ -532,7 +534,6 @@
     ]
     for load in loads[: 6 + 4]:
         load.start()
-    place.greet_all()
 
     def iota(shape, dim):
         return lax.broadcasted_iota(jnp.int32, shape, dim)

time: 182 us -> 182 us (level)
  no operation moved by 1% of the time
where the time goes in v5:
time: 182 us
  Pallas kernels  181 us (99%)
    pallas_call x1, Pallas kernels, layer(): pl.pallas_call(functools.partial(layer_kernel, (side, layers, cap, offset...  166 us
    pallas_call x1, Pallas kernels, spread(): pl.pallas_call(spread_kernel, out_shape=tuple((out for out, _ in outs)),...  15.5 us

profile of v5, /device:TPU:0, one launch (start us, length us, event | category | flops | bytes accessed | tf_op | source)
XLA Modules:
  0.0 182.2 jit_solution(15618343588874103294)
XLA Ops:
  0.7 165.9 %shard_map.349 = (bf16[256,768]{1,0:T(8,128)(2,1)}, f32[144,768]{1,0:T(8,128)}, bf16[25,2,2,4,48,384]{5,4,3,2,1,0:T(8,128)(2,1)}) custom-call(bf16[5,144,768]{2,1,0:T(8,128)(2,1)} %refs_0_.1, bf16[128,768]{1,0:T(8,128)(2,1)} %refs_1_.1, s32[1,256]{1,0:T(1,128)} %bitcast.5, s32[1,256]{1,0:T(1,128)} %bitcast.6, s32[1,256]{1,0:T(1,128)} %bitcast.7, s32[8]{0:T(128)} %refs_5_.1, ...), custom_call_target="tpu_custom_call" | custom-call | flops 10871635968 | bytes 41943040 | tf_op jit(solution)/shard_map/pallas_call | solution.py:872
  166.6 15.5 %shard_map.350 = (bf16[256,768]{1,0:T(8,128)(2,1)}, f32[5,144,768]{2,1,0:T(8,128)}, f32[128,768]{1,0:T(8,128)}, f32[768]{0:T(1024)}, f32[768]{0:T(1024)}, /*inde...) custom-call(bf16[25,768,384]{2,1,0:T(8,128)(2,1)} %bitcast.4, ...), custom_call_target="tpu_custom_call" | custom-call | bytes 50331648 | tf_op jit(solution)/shard_map/pallas_call | solution.py:1009
